TPU v7x, 1024 devices: a whole 4x4x32 slice. The times are simulated.
1024 devices in a mesh: lon: 64 (over y, z_hi, x), lat: 16 (over z_lo, core).
Axes of the slice: x: 4, y: 4, z: 32 (z_hi: 4, z_lo: 8; z = z_hi * 8 + z_lo), core: 2. Of those that a mesh axis runs over, the one named last changes fastest.
Arguments:
- tracers: float32 [2, 8, 768, 8192], P(None, None, 'lat', 'lon'), may hold values from -6 to 6
- east_courant: float32 [8, 768, 8192], P(None, 'lat', 'lon'), may hold values from -0.25 to 0.25
- north_courant: float32 [8, 768, 8192], P(None, 'lat', 'lon'), may hold values from -0.25 to 0.25
- diffusivity: float32 [8, 768, 8192], P(None, 'lat', 'lon'), may hold values from 0.01 to 0.12
- wet_levels: int32 [768, 8192], P('lat', 'lon'), may hold values from 0 to 8
Outputs:
- advected: float32 [2, 8, 768, 8192], P(None, None, 'lat', 'lon')
All inputs are finite; a program needn't handle non-finite values.
Results may differ from a plain program's by a relative error of at most 0.0003.
Values sent between devices are 32-bit elements; how exact they have to be, the bound alone decides.
A program may use at most 32 MiB of HBM per device.

v0:
```python
import jax
import jax.numpy as jnp
from jax import lax
from jax.sharding import PartitionSpec as P

STEPS = 3


def from_partner(shard, axis, stride):
    return lax.ppermute(shard, axis, [(i, i ^ 1 << stride) for i in range(lax.axis_size(axis))])


def padded(shard, sides, width, wrap):
    for axis, dim in sides:
        size, length = (lax.axis_size(axis), shard.shape[dim])
        up = [(i, (i + 1) % size) for i in range(size if wrap else size - 1)]
        down = [(j, i) for i, j in up]
        last = lax.slice_in_dim(shard, length - width, length, axis=dim)
        leading = lax.slice_in_dim(shard, 0, width, axis=dim)
        before = lax.ppermute(last, axis, up)
        after = lax.ppermute(leading, axis, down)
        shard = jnp.concatenate([before, shard, after], axis=dim)
    return shard


def minmod(first, second):
    return 0.5 * (jnp.sign(first) + jnp.sign(second)) * jnp.minimum(jnp.abs(first), jnp.abs(second))


def face_flux(behind, left_cell, right_cell, beyond, courant, face_kappa, face_mask):
    difference = right_cell - left_cell
    forward = courant > 0
    upwind = jnp.where(forward, left_cell, right_cell)
    upslope = jnp.where(forward, left_cell - behind, beyond - right_cell)
    magnitude = jnp.abs(courant)
    limited = minmod(difference, upslope)
    return (
        courant * upwind + 0.5 * magnitude * (1.0 - magnitude) * limited - face_kappa * difference
    ) * face_mask


def per_device(tracers, east_courant, north_courant, diffusivity, wet_levels):
    level_count = east_courant.shape[0]
    row_count = tracers.shape[2]
    col_count = tracers.shape[3]
    at_top = lax.axis_index("lat") == lax.axis_size("lat") - 1

    def mirror(edge_rows):
        moving = edge_rows
        for bit_number in range(lax.axis_size("lon").bit_length() - 1):
            moving = from_partner(moving, "lon", bit_number)
        result = moving[:, :, ::-1]
        return result

    def rims(field, skipped):
        zonal = padded(field, (("lon", 2),), 2, True)
        meridional = padded(field, (("lat", 1),), 2, False)
        folded = mirror(field[skipped:, ::-1][:, :2])
        if skipped > 0:
            folded = jnp.concatenate([jnp.zeros((skipped, 2, col_count), jnp.float32), folded], 0)
        northern = jnp.where(at_top, folded, meridional[:, row_count + 2 :])
        return (zonal, jnp.concatenate([meridional[:, : row_count + 2], northern], 1))

    statics = jnp.concatenate(
        [east_courant, north_courant, diffusivity, wet_levels.astype(jnp.float32)[None]], 0
    )
    static_zonal, static_merid = rims(statics, level_count)
    layers = jnp.arange(level_count, dtype=jnp.float32)[:, None, None]
    wet_zonal = (layers < static_zonal[3 * level_count][None]).astype(jnp.float32)
    east_speed = static_zonal[0:level_count, :, 1 : col_count + 2]
    kappa_zonal = static_zonal[2 * level_count : 3 * level_count]
    east_kappa = 0.5 * (kappa_zonal[:, :, 1 : col_count + 2] + kappa_zonal[:, :, 2 : col_count + 3])
    east_mask = wet_zonal[:, :, 1 : col_count + 2] * wet_zonal[:, :, 2 : col_count + 3]
    speed_rows = static_merid[level_count : 2 * level_count]
    fold_speed = 0.5 * (speed_rows[:, row_count + 1] - speed_rows[:, row_count + 2])
    last_speed = jnp.where(at_top, fold_speed, speed_rows[:, row_count + 1])
    north_speed = jnp.concatenate([speed_rows[:, 1 : row_count + 1], last_speed[:, None]], 1)
    kappa_merid = static_merid[2 * level_count : 3 * level_count]
    north_kappa = 0.5 * (kappa_merid[:, 1 : row_count + 2] + kappa_merid[:, 2 : row_count + 3])
    wet_merid = (layers < static_merid[3 * level_count][None]).astype(jnp.float32)
    north_mask = wet_merid[:, 1 : row_count + 2] * wet_merid[:, 2 : row_count + 3]
    current = tracers
    for repeat in range(STEPS):
        zonal, meridional = rims(current.reshape(2 * level_count, row_count, col_count), 0)
        zonal = zonal.reshape(2, level_count, row_count, col_count + 4)
        meridional = meridional.reshape(2, level_count, row_count + 4, col_count)
        east_flux = face_flux(
            zonal[:, :, :, 0 : col_count + 1],
            zonal[:, :, :, 1 : col_count + 2],
            zonal[:, :, :, 2 : col_count + 3],
            zonal[:, :, :, 3 : col_count + 4],
            east_speed,
            east_kappa,
            east_mask,
        )
        north_flux = face_flux(
            meridional[:, :, 0 : row_count + 1],
            meridional[:, :, 1 : row_count + 2],
            meridional[:, :, 2 : row_count + 3],
            meridional[:, :, 3 : row_count + 4],
            north_speed,
            north_kappa,
            north_mask,
        )
        current = (
            current
            - (east_flux[:, :, :, 1:] - east_flux[:, :, :, :-1])
            - (north_flux[:, :, 1:] - north_flux[:, :, :-1])
        )
    return current


def solution(mesh):
    placed = (
        P(None, None, "lat", "lon"),
        P(None, "lat", "lon"),
        P(None, "lat", "lon"),
        P(None, "lat", "lon"),
        P("lat", "lon"),
    )
    return jax.shard_map(
        per_device,
        mesh=mesh,
        in_specs=placed,
        out_specs=P(None, None, "lat", "lon"),
        check_vma=False,
    )
```

profile of v0, /device:TPU:87, one launch (start us, length us, event | category | flops | bytes accessed | tf_op | source)
XLA Modules:
  0.0 457.4 jit_solution(8560000054694480717)
XLA Ops:
  5.0 4.4 collective-permute-start.12
  12.9 15.5 %collective-permute-start = (f32[25,48,2]{1,0,2:T(8,128)S(1)}, f32[25,48,2]{1,0,2:T(8,128)S(1)}, u32[]{:S(2)}, u32[]{:S(2)}) collective-permute-start(f32[25,48,2]{1,0,2:T(8,128)S(1)} %copy.27), channel_id=1, source_target_pairs={{0,16},{16,32},{32,48},{48,64},{64,80},{80,96},{96,112},{112,128},... | collective-permute-start | bytes 28808 | tf_op jit(solution)/shard_map/ppermute | solution.py:20
  31.7 14.2 %collective-permute-start.1 = (f32[16,48,2]{2,1,0:T(8,128)}, f32[16,48,2]{2,1,0:T(8,128)}, u32[]{:S(2)}, u32[]{:S(2)}) collective-permute-start(f32[16,48,2]{2,1,0:T(8,128)} %get-tuple-element.21), channel_id=1, source_target_pairs={{0,16},{16,32},{32,48},{48,64},{64,80},{80,96},{96,112},{112,128},... | collective-permute-start | bytes 18440 | tf_op jit(solution)/shard_map/ppermute | solution.py:20
  51.5 4.9 %collective-permute-start.6 = (f32[17,2,128]{2,1,0:T(2,128)S(1)}, f32[17,2,128]{2,1,0:T(2,128)S(1)}, u32[]{:S(2)}, u32[]{:S(2)}) collective-permute-start(f32[17,2,128]{2,1,0:T(2,128)S(1)} %collective-permute-done.5), channel_id=1, source_target_pairs={{0,32},{16,48},{32,0},{48,16},{64,96},{80,112},{96,64},{112,80},{1... | collective-permute-start | bytes 52232 | tf_op jit(solution)/shard_map/ppermute | solution.py:10
  57.6 15.0 %collective-permute-start.15 = (f32[16,2,128]{2,1,0:T(2,128)S(1)}, f32[16,2,128]{2,1,0:T(2,128)S(1)}, u32[]{:S(2)}, u32[]{:S(2)}) collective-permute-start(f32[16,2,128]{2,1,0:T(2,128)S(1)} %collective-permute-done.14), channel_id=1, source_target_pairs={{0,64},{16,80},{32,96},{48,112},{64,0},{80,16},{96,32},{112,48},{1... | collective-permute-start | bytes 49160 | tf_op jit(solution)/shard_map/ppermute | solution.py:10
  74.9 29.2 %collective-permute-done.15 = f32[16,2,128]{2,1,0:T(2,128)S(1)} collective-permute-done((f32[16,2,128]{2,1,0:T(2,128)S(1)}, f32[16,2,128]{2,1,0:T(2,128)S(1)}, u32[]{:S(2)}, u32[]{:S(2)}) %collective-permute-start.15) | collective-permute-done | bytes 16416 | tf_op jit(solution)/shard_map/ppermute | solution.py:10
  104.0 20.3 %collective-permute-start.16 = (f32[16,2,128]{2,1,0:T(2,128)S(1)}, f32[16,2,128]{2,1,0:T(2,128)S(1)}, u32[]{:S(2)}, u32[]{:S(2)}) collective-permute-start(f32[16,2,128]{2,1,0:T(2,128)S(1)} %collective-permute-done.15), channel_id=1, source_target_pairs={{0,128},{16,144},{32,160},{48,176},{64,192},{80,208},{96,224},{112... | collective-permute-start | bytes 49160 | tf_op jit(solution)/shard_map/ppermute | solution.py:10
  124.4 3.3 collective-permute-start.8
  129.2 8.8 %collective-permute-start.17 = (f32[16,2,128]{2,1,0:T(2,128)S(1)}, f32[16,2,128]{2,1,0:T(2,128)S(1)}, u32[]{:S(2)}, u32[]{:S(2)}) collective-permute-start(f32[16,2,128]{2,1,0:T(2,128)S(1)} %collective-permute-done.16), channel_id=1, source_target_pairs={{0,256},{16,272},{32,288},{48,304},{64,320},{80,336},{96,352},{112... | collective-permute-start | bytes 49160 | tf_op jit(solution)/shard_map/ppermute | solution.py:10
  142.8 4.5 collective-permute-done.8
  147.3 4.0 collective-permute-start.9
  153.3 3.3 subtract_multiply_fusion.2
  156.6 14.6 %collective-permute-start.4 = (f32[25,2,128]{2,1,0:T(2,128)S(1)}, f32[25,2,128]{2,1,0:T(2,128)S(1)}, u32[]{:S(2)}, u32[]{:S(2)}) collective-permute-start(f32[25,2,128]{2,1,0:T(2,128)S(1)} %get-tuple-element.11), channel_id=1, source_target_pairs={{0,1},{1,2},{2,3},{3,4},{4,5},{5,6},{6,7},{7,8},{8,9},{9,10},{10,1... | collective-permute-start | bytes 76808 | tf_op jit(solution)/shard_map/ppermute | solution.py:20
  171.2 4.2 collective-permute-start.10
  184.1 16.9 %collective-permute-start.24 = (f32[16,2,128]{2,1,0:T(2,128)S(1)}, f32[16,2,128]{2,1,0:T(2,128)S(1)}, u32[]{:S(2)}, u32[]{:S(2)}) collective-permute-start(f32[16,2,128]{2,1,0:T(2,128)S(1)} %collective-permute-done.23), channel_id=1, source_target_pairs={{0,32},{16,48},{32,0},{48,16},{64,96},{80,112},{96,64},{112,80},{1... | collective-permute-start | bytes 49160 | tf_op jit(solution)/shard_map/ppermute | solution.py:10
  204.1 11.3 %collective-permute-done.25 = f32[16,2,128]{2,1,0:T(2,128)S(1)} collective-permute-done((f32[16,2,128]{2,1,0:T(2,128)S(1)}, f32[16,2,128]{2,1,0:T(2,128)S(1)}, u32[]{:S(2)}, u32[]{:S(2)}) %collective-permute-start.25) | collective-permute-done | bytes 16416 | tf_op jit(solution)/shard_map/ppermute | solution.py:10
  215.3 9.2 %collective-permute-start.26 = (f32[16,2,128]{2,1,0:T(2,128)S(1)}, f32[16,2,128]{2,1,0:T(2,128)S(1)}, u32[]{:S(2)}, u32[]{:S(2)}) collective-permute-start(f32[16,2,128]{2,1,0:T(2,128)S(1)} %collective-permute-done.25), channel_id=1, source_target_pairs={{0,128},{16,144},{32,160},{48,176},{64,192},{80,208},{96,224},{112... | collective-permute-start | bytes 49160 | tf_op jit(solution)/shard_map/ppermute | solution.py:10
  224.5 13.6 %collective-permute-done.26 = f32[16,2,128]{2,1,0:T(2,128)S(1)} collective-permute-done((f32[16,2,128]{2,1,0:T(2,128)S(1)}, f32[16,2,128]{2,1,0:T(2,128)S(1)}, u32[]{:S(2)}, u32[]{:S(2)}) %collective-permute-start.26) | collective-permute-done | bytes 16416 | tf_op jit(solution)/shard_map/ppermute | solution.py:10
  243.6 13.2 %collective-permute-start.20 = (f32[16,48,2]{2,1,0:T(8,128)S(1)}, f32[16,48,2]{2,1,0:T(8,128)S(1)}, u32[]{:S(2)}, u32[]{:S(2)}) collective-permute-start(f32[16,48,2]{2,1,0:T(8,128)S(1)} %get-tuple-element.17), channel_id=1, source_target_pairs={{0,16},{16,32},{32,48},{48,64},{64,80},{80,96},{96,112},{112,128},... | collective-permute-start | bytes 18440 | tf_op jit(solution)/shard_map/ppermute | solution.py:20
  256.8 7.9 %collective-permute-start.22 = (f32[16,2,128]{2,1,0:T(2,128)S(1)}, f32[16,2,128]{2,1,0:T(2,128)S(1)}, u32[]{:S(2)}, u32[]{:S(2)}) collective-permute-start(f32[16,2,128]{2,1,0:T(2,128)S(1)} %get-tuple-element.20), channel_id=1, source_target_pairs={{0,1},{1,2},{2,3},{3,4},{4,5},{5,6},{6,7},{7,8},{8,9},{9,10},{10,1... | collective-permute-start | bytes 49160 | tf_op jit(solution)/shard_map/ppermute | solution.py:20
  267.8 3.2 collective-permute-start.28
  271.0 36.9 %collective-permute-done.21 = f32[16,48,2]{2,1,0:T(8,128)S(1)} collective-permute-done((f32[16,48,2]{2,1,0:T(8,128)S(1)}, f32[16,48,2]{2,1,0:T(8,128)S(1)}, u32[]{:S(2)}, u32[]{:S(2)}) %collective-permute-start.21) | collective-permute-done | bytes 6176 | tf_op jit(solution)/shard_map/ppermute | solution.py:21
  307.9 8.8 %collective-permute-done.20 = f32[16,48,2]{2,1,0:T(8,128)S(1)} collective-permute-done((f32[16,48,2]{2,1,0:T(8,128)S(1)}, f32[16,48,2]{2,1,0:T(8,128)S(1)}, u32[]{:S(2)}, u32[]{:S(2)}) %collective-permute-start.20) | collective-permute-done | bytes 6176 | tf_op jit(solution)/shard_map/ppermute | solution.py:20
  324.8 9.2 %collective-permute-start.34 = (f32[16,2,128]{2,1,0:T(2,128)S(1)}, f32[16,2,128]{2,1,0:T(2,128)S(1)}, u32[]{:S(2)}, u32[]{:S(2)}) collective-permute-start(f32[16,2,128]{2,1,0:T(2,128)S(1)} %collective-permute-done.33), channel_id=1, source_target_pairs={{0,32},{16,48},{32,0},{48,16},{64,96},{80,112},{96,64},{112,80},{1... | collective-permute-start | bytes 49160 | tf_op jit(solution)/shard_map/ppermute | solution.py:10
  335.1 7.6 %collective-permute-start.35 = (f32[16,2,128]{2,1,0:T(2,128)S(1)}, f32[16,2,128]{2,1,0:T(2,128)S(1)}, u32[]{:S(2)}, u32[]{:S(2)}) collective-permute-start(f32[16,2,128]{2,1,0:T(2,128)S(1)} %collective-permute-done.34), channel_id=1, source_target_pairs={{0,64},{16,80},{32,96},{48,112},{64,0},{80,16},{96,32},{112,48},{1... | collective-permute-start | bytes 49160 | tf_op jit(solution)/shard_map/ppermute | solution.py:10
  342.8 5.6 %collective-permute-done.35 = f32[16,2,128]{2,1,0:T(2,128)S(1)} collective-permute-done((f32[16,2,128]{2,1,0:T(2,128)S(1)}, f32[16,2,128]{2,1,0:T(2,128)S(1)}, u32[]{:S(2)}, u32[]{:S(2)}) %collective-permute-start.35) | collective-permute-done | bytes 16416 | tf_op jit(solution)/shard_map/ppermute | solution.py:10
  348.3 13.4 %collective-permute-start.36 = (f32[16,2,128]{2,1,0:T(2,128)S(1)}, f32[16,2,128]{2,1,0:T(2,128)S(1)}, u32[]{:S(2)}, u32[]{:S(2)}) collective-permute-start(f32[16,2,128]{2,1,0:T(2,128)S(1)} %collective-permute-done.35), channel_id=1, source_target_pairs={{0,128},{16,144},{32,160},{48,176},{64,192},{80,208},{96,224},{112... | collective-permute-start | bytes 49160 | tf_op jit(solution)/shard_map/ppermute | solution.py:10
  361.8 9.6 %collective-permute-done.36 = f32[16,2,128]{2,1,0:T(2,128)S(1)} collective-permute-done((f32[16,2,128]{2,1,0:T(2,128)S(1)}, f32[16,2,128]{2,1,0:T(2,128)S(1)}, u32[]{:S(2)}, u32[]{:S(2)}) %collective-permute-start.36) | collective-permute-done | bytes 16416 | tf_op jit(solution)/shard_map/ppermute | solution.py:10
  374.6 12.0 %collective-permute-start.30 = (f32[16,48,2]{2,1,0:T(8,128)S(1)}, f32[16,48,2]{2,1,0:T(8,128)S(1)}, u32[]{:S(2)}, u32[]{:S(2)}) collective-permute-start(f32[16,48,2]{2,1,0:T(8,128)S(1)} %get-tuple-element.13), channel_id=1, source_target_pairs={{0,16},{16,32},{32,48},{48,64},{64,80},{80,96},{96,112},{112,128},... | collective-permute-start | bytes 18440 | tf_op jit(solution)/shard_map/ppermute | solution.py:20
  390.6 8.2 %collective-permute-start.39 = (f32[16,2,128]{2,1,0:T(2,128)S(1)}, f32[16,2,128]{2,1,0:T(2,128)S(1)}, u32[]{:S(2)}, u32[]{:S(2)}) collective-permute-start(f32[16,2,128]{2,1,0:T(2,128)S(1)} %get-tuple-element.15), channel_id=1, source_target_pairs={{1,0},{2,1},{3,2},{4,3},{5,4},{6,5},{7,6},{8,7},{9,8},{10,9},{11,1... | collective-permute-start | bytes 49160 | tf_op jit(solution)/shard_map/ppermute | solution.py:21
  401.7 11.8 %collective-permute-done.30 = f32[16,48,2]{2,1,0:T(8,128)S(1)} collective-permute-done((f32[16,48,2]{2,1,0:T(8,128)S(1)}, f32[16,48,2]{2,1,0:T(8,128)S(1)}, u32[]{:S(2)}, u32[]{:S(2)}) %collective-permute-start.30) | collective-permute-done | bytes 6176 | tf_op jit(solution)/shard_map/ppermute | solution.py:20
  413.4 39.7 %collective-permute-done.31 = f32[16,48,2]{2,1,0:T(8,128)S(1)} collective-permute-done((f32[16,48,2]{2,1,0:T(8,128)S(1)}, f32[16,48,2]{2,1,0:T(8,128)S(1)}, u32[]{:S(2)}, u32[]{:S(2)}) %collective-permute-start.31) | collective-permute-done | bytes 6176 | tf_op jit(solution)/shard_map/ppermute | solution.py:21
  (122 shorter events, 72.5 us)
Async XLA Ops:
  1.7 49.8 %collective-permute-start.5 = (f32[17,2,128]{2,1,0:T(2,128)S(1)}, f32[17,2,128]{2,1,0:T(2,128)S(1)}, u32[]{:S(2)}, u32[]{:S(2)}) collective-permute-start(f32[17,2,128]{2,1,0:T(2,128)S(1)} %slice.282), channel_id=1, source_target_pairs={{0,16},{16,0},{32,48},{48,32},{64,80},{80,64},{96,112},{112,96},{1... | collective-permute-start | bytes 52232 | tf_op jit(solution)/shard_map/ppermute | solution.py:10
  5.0 172.6 %collective-permute-start.12 = (f32[16,2,128]{2,1,0:T(2,128)S(1)}, f32[16,2,128]{2,1,0:T(2,128)S(1)}, u32[]{:S(2)}, u32[]{:S(2)}) collective-permute-start(f32[16,2,128]{2,1,0:T(2,128)S(1)} %get-tuple-element.24), channel_id=1, source_target_pairs={{0,1},{1,2},{2,3},{3,4},{4,5},{5,6},{6,7},{7,8},{8,9},{9,10},{10,1... | collective-permute-start | bytes 49160 | tf_op jit(solution)/shard_map/ppermute | solution.py:20
  9.5 39.8 %collective-permute-start.13 = (f32[16,2,128]{2,1,0:T(2,128)S(1)}, f32[16,2,128]{2,1,0:T(2,128)S(1)}, u32[]{:S(2)}, u32[]{:S(2)}) collective-permute-start(f32[16,2,128]{2,1,0:T(2,128)S(1)} %slice.287), channel_id=1, source_target_pairs={{0,16},{16,0},{32,48},{48,32},{64,80},{80,64},{96,112},{112,96},{1... | collective-permute-start | bytes 49160 | tf_op jit(solution)/shard_map/ppermute | solution.py:10
  12.9 18.8 %collective-permute-start = (f32[25,48,2]{1,0,2:T(8,128)S(1)}, f32[25,48,2]{1,0,2:T(8,128)S(1)}, u32[]{:S(2)}, u32[]{:S(2)}) collective-permute-start(f32[25,48,2]{1,0,2:T(8,128)S(1)} %copy.27), channel_id=1, source_target_pairs={{0,16},{16,32},{32,48},{48,64},{64,80},{80,96},{96,112},{112,128},... | collective-permute-start | bytes 28808 | tf_op jit(solution)/shard_map/ppermute | solution.py:20
  28.7 17.5 %collective-permute-start.3 = (f32[25,48,2]{1,0,2:T(8,128)S(1)}, f32[25,48,2]{1,0,2:T(8,128)S(1)}, u32[]{:S(2)}, u32[]{:S(2)}) collective-permute-start(f32[25,48,2]{1,0,2:T(8,128)S(1)} %copy.29), channel_id=1, source_target_pairs={{16,0},{32,16},{48,32},{64,48},{80,64},{96,80},{112,96},{128,112},... | collective-permute-start | bytes 28808 | tf_op jit(solution)/shard_map/ppermute | solution.py:21
  31.7 106.5 %collective-permute-start.1 = (f32[16,48,2]{2,1,0:T(8,128)}, f32[16,48,2]{2,1,0:T(8,128)}, u32[]{:S(2)}, u32[]{:S(2)}) collective-permute-start(f32[16,48,2]{2,1,0:T(8,128)} %get-tuple-element.21), channel_id=1, source_target_pairs={{0,16},{16,32},{32,48},{48,64},{64,80},{80,96},{96,112},{112,128},... | collective-permute-start | bytes 18440 | tf_op jit(solution)/shard_map/ppermute | solution.py:20
  46.2 94.7 %collective-permute-start.2 = (f32[16,48,2]{2,1,0:T(8,128)}, f32[16,48,2]{2,1,0:T(8,128)}, u32[]{:S(2)}, u32[]{:S(2)}) collective-permute-start(f32[16,48,2]{2,1,0:T(8,128)} %get-tuple-element.22), channel_id=1, source_target_pairs={{16,0},{32,16},{48,32},{64,48},{80,64},{96,80},{112,96},{128,112},... | collective-permute-start | bytes 18440 | tf_op jit(solution)/shard_map/ppermute | solution.py:21
  51.5 21.3 %collective-permute-start.6 = (f32[17,2,128]{2,1,0:T(2,128)S(1)}, f32[17,2,128]{2,1,0:T(2,128)S(1)}, u32[]{:S(2)}, u32[]{:S(2)}) collective-permute-start(f32[17,2,128]{2,1,0:T(2,128)S(1)} %collective-permute-done.5), channel_id=1, source_target_pairs={{0,32},{16,48},{32,0},{48,16},{64,96},{80,112},{96,64},{112,80},{1... | collective-permute-start | bytes 52232 | tf_op jit(solution)/shard_map/ppermute | solution.py:10
  57.6 46.4 %collective-permute-start.15 = (f32[16,2,128]{2,1,0:T(2,128)S(1)}, f32[16,2,128]{2,1,0:T(2,128)S(1)}, u32[]{:S(2)}, u32[]{:S(2)}) collective-permute-start(f32[16,2,128]{2,1,0:T(2,128)S(1)} %collective-permute-done.14), channel_id=1, source_target_pairs={{0,64},{16,80},{32,96},{48,112},{64,0},{80,16},{96,32},{112,48},{1... | collective-permute-start | bytes 49160 | tf_op jit(solution)/shard_map/ppermute | solution.py:10
  72.8 51.6 %collective-permute-start.7 = (f32[17,2,128]{2,1,0:T(2,128)S(1)}, f32[17,2,128]{2,1,0:T(2,128)S(1)}, u32[]{:S(2)}, u32[]{:S(2)}) collective-permute-start(f32[17,2,128]{2,1,0:T(2,128)S(1)} %collective-permute-done.6), channel_id=1, source_target_pairs={{0,64},{16,80},{32,96},{48,112},{64,0},{80,16},{96,32},{112,48},{1... | collective-permute-start | bytes 52232 | tf_op jit(solution)/shard_map/ppermute | solution.py:10
  104.0 25.2 %collective-permute-start.16 = (f32[16,2,128]{2,1,0:T(2,128)S(1)}, f32[16,2,128]{2,1,0:T(2,128)S(1)}, u32[]{:S(2)}, u32[]{:S(2)}) collective-permute-start(f32[16,2,128]{2,1,0:T(2,128)S(1)} %collective-permute-done.15), channel_id=1, source_target_pairs={{0,128},{16,144},{32,160},{48,176},{64,192},{80,208},{96,224},{112... | collective-permute-start | bytes 49160 | tf_op jit(solution)/shard_map/ppermute | solution.py:10
  124.4 22.9 %collective-permute-start.8 = (f32[17,2,128]{2,1,0:T(2,128)S(1)}, f32[17,2,128]{2,1,0:T(2,128)S(1)}, u32[]{:S(2)}, u32[]{:S(2)}) collective-permute-start(f32[17,2,128]{2,1,0:T(2,128)S(1)} %collective-permute-done.7), channel_id=1, source_target_pairs={{0,128},{16,144},{32,160},{48,176},{64,192},{80,208},{96,224},{112... | collective-permute-start | bytes 52232 | tf_op jit(solution)/shard_map/ppermute | solution.py:10
  129.2 22.1 %collective-permute-start.17 = (f32[16,2,128]{2,1,0:T(2,128)S(1)}, f32[16,2,128]{2,1,0:T(2,128)S(1)}, u32[]{:S(2)}, u32[]{:S(2)}) collective-permute-start(f32[16,2,128]{2,1,0:T(2,128)S(1)} %collective-permute-done.16), channel_id=1, source_target_pairs={{0,256},{16,272},{32,288},{48,304},{64,320},{80,336},{96,352},{112... | collective-permute-start | bytes 49160 | tf_op jit(solution)/shard_map/ppermute | solution.py:10
  138.2 39.1 %collective-permute-start.11 = (f32[25,2,128]{2,1,0:T(2,128)S(1)}, f32[25,2,128]{2,1,0:T(2,128)S(1)}, u32[]{:S(2)}, u32[]{:S(2)}) collective-permute-start(f32[25,2,128]{2,1,0:T(2,128)S(1)} %get-tuple-element.12), channel_id=1, source_target_pairs={{1,0},{2,1},{3,2},{4,3},{5,4},{6,5},{7,6},{8,7},{9,8},{10,9},{11,1... | collective-permute-start | bytes 76808 | tf_op jit(solution)/shard_map/ppermute | solution.py:21
  140.9 34.6 %collective-permute-start.19 = (f32[16,2,128]{2,1,0:T(2,128)S(1)}, f32[16,2,128]{2,1,0:T(2,128)S(1)}, u32[]{:S(2)}, u32[]{:S(2)}) collective-permute-start(f32[16,2,128]{2,1,0:T(2,128)S(1)} %get-tuple-element.23), channel_id=1, source_target_pairs={{1,0},{2,1},{3,2},{4,3},{5,4},{6,5},{7,6},{8,7},{9,8},{10,9},{11,1... | collective-permute-start | bytes 49160 | tf_op jit(solution)/shard_map/ppermute | solution.py:21
  151.3 19.8 %collective-permute-start.18 = (f32[16,2,128]{2,1,0:T(2,128)S(1)}, f32[16,2,128]{2,1,0:T(2,128)S(1)}, u32[]{:S(2)}, u32[]{:S(2)}) collective-permute-start(f32[16,2,128]{2,1,0:T(2,128)S(1)} %collective-permute-done.17), channel_id=1, source_target_pairs={{0,512},{16,528},{32,544},{48,560},{64,576},{80,592},{96,608},{112... | collective-permute-start | bytes 49160 | tf_op jit(solution)/shard_map/ppermute | solution.py:10
  156.6 20.8 %collective-permute-start.4 = (f32[25,2,128]{2,1,0:T(2,128)S(1)}, f32[25,2,128]{2,1,0:T(2,128)S(1)}, u32[]{:S(2)}, u32[]{:S(2)}) collective-permute-start(f32[25,2,128]{2,1,0:T(2,128)S(1)} %get-tuple-element.11), channel_id=1, source_target_pairs={{0,1},{1,2},{2,3},{3,4},{4,5},{5,6},{6,7},{7,8},{8,9},{9,10},{10,1... | collective-permute-start | bytes 76808 | tf_op jit(solution)/shard_map/ppermute | solution.py:20
  184.1 18.1 %collective-permute-start.24 = (f32[16,2,128]{2,1,0:T(2,128)S(1)}, f32[16,2,128]{2,1,0:T(2,128)S(1)}, u32[]{:S(2)}, u32[]{:S(2)}) collective-permute-start(f32[16,2,128]{2,1,0:T(2,128)S(1)} %collective-permute-done.23), channel_id=1, source_target_pairs={{0,32},{16,48},{32,0},{48,16},{64,96},{80,112},{96,64},{112,80},{1... | collective-permute-start | bytes 49160 | tf_op jit(solution)/shard_map/ppermute | solution.py:10
  215.3 22.8 %collective-permute-start.26 = (f32[16,2,128]{2,1,0:T(2,128)S(1)}, f32[16,2,128]{2,1,0:T(2,128)S(1)}, u32[]{:S(2)}, u32[]{:S(2)}) collective-permute-start(f32[16,2,128]{2,1,0:T(2,128)S(1)} %collective-permute-done.25), channel_id=1, source_target_pairs={{0,128},{16,144},{32,160},{48,176},{64,192},{80,208},{96,224},{112... | collective-permute-start | bytes 49160 | tf_op jit(solution)/shard_map/ppermute | solution.py:10
  238.1 29.7 %collective-permute-start.27 = (f32[16,2,128]{2,1,0:T(2,128)S(1)}, f32[16,2,128]{2,1,0:T(2,128)S(1)}, u32[]{:S(2)}, u32[]{:S(2)}) collective-permute-start(f32[16,2,128]{2,1,0:T(2,128)S(1)} %collective-permute-done.26), channel_id=1, source_target_pairs={{0,256},{16,272},{32,288},{48,304},{64,320},{80,336},{96,352},{112... | collective-permute-start | bytes 49160 | tf_op jit(solution)/shard_map/ppermute | solution.py:10
  240.7 67.2 %collective-permute-start.21 = (f32[16,48,2]{2,1,0:T(8,128)S(1)}, f32[16,48,2]{2,1,0:T(8,128)S(1)}, u32[]{:S(2)}, u32[]{:S(2)}) collective-permute-start(f32[16,48,2]{2,1,0:T(8,128)S(1)} %get-tuple-element.18), channel_id=1, source_target_pairs={{16,0},{32,16},{48,32},{64,48},{80,64},{96,80},{112,96},{128,112},... | collective-permute-start | bytes 18440 | tf_op jit(solution)/shard_map/ppermute | solution.py:21
  243.6 73.2 %collective-permute-start.20 = (f32[16,48,2]{2,1,0:T(8,128)S(1)}, f32[16,48,2]{2,1,0:T(8,128)S(1)}, u32[]{:S(2)}, u32[]{:S(2)}) collective-permute-start(f32[16,48,2]{2,1,0:T(8,128)S(1)} %get-tuple-element.17), channel_id=1, source_target_pairs={{0,16},{16,32},{32,48},{48,64},{64,80},{80,96},{96,112},{112,128},... | collective-permute-start | bytes 18440 | tf_op jit(solution)/shard_map/ppermute | solution.py:20
  256.8 62.1 %collective-permute-start.22 = (f32[16,2,128]{2,1,0:T(2,128)S(1)}, f32[16,2,128]{2,1,0:T(2,128)S(1)}, u32[]{:S(2)}, u32[]{:S(2)}) collective-permute-start(f32[16,2,128]{2,1,0:T(2,128)S(1)} %get-tuple-element.20), channel_id=1, source_target_pairs={{0,1},{1,2},{2,3},{3,4},{4,5},{5,6},{6,7},{7,8},{8,9},{9,10},{10,1... | collective-permute-start | bytes 49160 | tf_op jit(solution)/shard_map/ppermute | solution.py:20
  264.8 54.1 %collective-permute-start.29 = (f32[16,2,128]{2,1,0:T(2,128)S(1)}, f32[16,2,128]{2,1,0:T(2,128)S(1)}, u32[]{:S(2)}, u32[]{:S(2)}) collective-permute-start(f32[16,2,128]{2,1,0:T(2,128)S(1)} %get-tuple-element.19), channel_id=1, source_target_pairs={{1,0},{2,1},{3,2},{4,3},{5,4},{6,5},{7,6},{8,7},{9,8},{10,9},{11,1... | collective-permute-start | bytes 49160 | tf_op jit(solution)/shard_map/ppermute | solution.py:21
  267.8 50.9 %collective-permute-start.28 = (f32[16,2,128]{2,1,0:T(2,128)S(1)}, f32[16,2,128]{2,1,0:T(2,128)S(1)}, u32[]{:S(2)}, u32[]{:S(2)}) collective-permute-start(f32[16,2,128]{2,1,0:T(2,128)S(1)} %collective-permute-done.27), channel_id=1, source_target_pairs={{0,512},{16,528},{32,544},{48,560},{64,576},{80,592},{96,608},{112... | collective-permute-start | bytes 49160 | tf_op jit(solution)/shard_map/ppermute | solution.py:10
  348.3 23.1 %collective-permute-start.36 = (f32[16,2,128]{2,1,0:T(2,128)S(1)}, f32[16,2,128]{2,1,0:T(2,128)S(1)}, u32[]{:S(2)}, u32[]{:S(2)}) collective-permute-start(f32[16,2,128]{2,1,0:T(2,128)S(1)} %collective-permute-done.35), channel_id=1, source_target_pairs={{0,128},{16,144},{32,160},{48,176},{64,192},{80,208},{96,224},{112... | collective-permute-start | bytes 49160 | tf_op jit(solution)/shard_map/ppermute | solution.py:10
  371.4 27.5 %collective-permute-start.37 = (f32[16,2,128]{2,1,0:T(2,128)S(1)}, f32[16,2,128]{2,1,0:T(2,128)S(1)}, u32[]{:S(2)}, u32[]{:S(2)}) collective-permute-start(f32[16,2,128]{2,1,0:T(2,128)S(1)} %collective-permute-done.36), channel_id=1, source_target_pairs={{0,256},{16,272},{32,288},{48,304},{64,320},{80,336},{96,352},{112... | collective-permute-start | bytes 49160 | tf_op jit(solution)/shard_map/ppermute | solution.py:10
  374.6 38.9 %collective-permute-start.30 = (f32[16,48,2]{2,1,0:T(8,128)S(1)}, f32[16,48,2]{2,1,0:T(8,128)S(1)}, u32[]{:S(2)}, u32[]{:S(2)}) collective-permute-start(f32[16,48,2]{2,1,0:T(8,128)S(1)} %get-tuple-element.13), channel_id=1, source_target_pairs={{0,16},{16,32},{32,48},{48,64},{64,80},{80,96},{96,112},{112,128},... | collective-permute-start | bytes 18440 | tf_op jit(solution)/shard_map/ppermute | solution.py:20
  386.6 66.5 %collective-permute-start.31 = (f32[16,48,2]{2,1,0:T(8,128)S(1)}, f32[16,48,2]{2,1,0:T(8,128)S(1)}, u32[]{:S(2)}, u32[]{:S(2)}) collective-permute-start(f32[16,48,2]{2,1,0:T(8,128)S(1)} %get-tuple-element.14), channel_id=1, source_target_pairs={{16,0},{32,16},{48,32},{64,48},{80,64},{96,80},{112,96},{128,112},... | collective-permute-start | bytes 18440 | tf_op jit(solution)/shard_map/ppermute | solution.py:21
  388.5 66.8 %collective-permute-start.32 = (f32[16,2,128]{2,1,0:T(2,128)S(1)}, f32[16,2,128]{2,1,0:T(2,128)S(1)}, u32[]{:S(2)}, u32[]{:S(2)}) collective-permute-start(f32[16,2,128]{2,1,0:T(2,128)S(1)} %get-tuple-element.16), channel_id=1, source_target_pairs={{0,1},{1,2},{2,3},{3,4},{4,5},{5,6},{6,7},{7,8},{8,9},{9,10},{10,1... | collective-permute-start | bytes 49160 | tf_op jit(solution)/shard_map/ppermute | solution.py:20
  390.6 64.6 %collective-permute-start.39 = (f32[16,2,128]{2,1,0:T(2,128)S(1)}, f32[16,2,128]{2,1,0:T(2,128)S(1)}, u32[]{:S(2)}, u32[]{:S(2)}) collective-permute-start(f32[16,2,128]{2,1,0:T(2,128)S(1)} %get-tuple-element.15), channel_id=1, source_target_pairs={{1,0},{2,1},{3,2},{4,3},{5,4},{6,5},{7,6},{8,7},{9,8},{10,9},{11,1... | collective-permute-start | bytes 49160 | tf_op jit(solution)/shard_map/ppermute | solution.py:21
  398.8 56.3 %collective-permute-start.38 = (f32[16,2,128]{2,1,0:T(2,128)S(1)}, f32[16,2,128]{2,1,0:T(2,128)S(1)}, u32[]{:S(2)}, u32[]{:S(2)}) collective-permute-start(f32[16,2,128]{2,1,0:T(2,128)S(1)} %collective-permute-done.37), channel_id=1, source_target_pairs={{0,512},{16,528},{32,544},{48,560},{64,576},{80,592},{96,608},{112... | collective-permute-start | bytes 49160 | tf_op jit(solution)/shard_map/ppermute | solution.py:10
  (21 other events, 338.1 us)
where the time goes:
time: 459 us; the launch traced here: 457 us
  starting transfers between devices  253 us (55%)
  waiting for transfers between devices  183 us (40%)
  other arithmetic  13.3 us (3%)
  local copies, waits for them, and re-layouts  7.18 us (2%)
    ppermute x24, starting transfers between devices, from_partner(): lax.ppermute(shard, axis, [(i, i ^ 1 << stride) for i in range(lax.axis_s...  145 us
    ppermute x24, waiting for transfers between devices, from_partner(): lax.ppermute(shard, axis, [(i, i ^ 1 << stride) for i in range(lax.axis_s...  85.5 us
    ppermute x8, starting transfers between devices, padded(): before = lax.ppermute(last, axis, up)  84 us
    ppermute x8, waiting for transfers between devices, padded(): after = lax.ppermute(leading, axis, down)  76.6 us
    ppermute x8, starting transfers between devices, padded(): after = lax.ppermute(leading, axis, down)  24.4 us
    ppermute x8, waiting for transfers between devices, padded(): before = lax.ppermute(last, axis, up)  20.6 us
  transfers between devices with their start and end apart: 40, of which 17 were waited for; matrix products, arithmetic and copies ran while one was open for 3% of the time, Pallas kernels for 0%

commit v1 on v0

v1 whole, which is shorter than its diff:
```python
import functools

import jax
import jax.numpy as jnp
from jax import lax
from jax.experimental import pallas as pl
from jax.experimental.pallas import tpu as pltpu
from jax.sharding import PartitionSpec as P

MESH = pl.DeviceIdType.MESH
LEVELS, ROWS, COLS = 8, 48, 128
PAD = 8
SPAN = ROWS + 2 * PAD
REACH = 6
UNROLL = 4
T0, T1, EAST, NORTH, KAPPA, WET = range(6)
SLOTS = ((6, 6), (6, 12), (5, 17), (4, 21), (5, 26), (5, 31))


def roll(value, shift):
    return pltpu.roll(value, shift % COLS, 1)


def lane_index():
    return lax.broadcasted_iota(jnp.int32, (LEVELS, COLS), 1)


def reverse(value):
    return jnp.take_along_axis(value, COLS - 1 - lane_index(), axis=1, mode="promise_in_bounds")


def face(speed, kappa_sum, mask):
    speed = speed * mask
    magnitude = jnp.abs(speed)
    return (
        speed,
        jnp.minimum(speed, 0.0) - 0.5 * kappa_sum * mask,
        0.5 * magnitude * (1.0 - magnitude),
    )


def flux(cell, before, here, after, coef):
    speed, drift, limit = coef
    upslope = jnp.where(speed > 0, before, after)
    limited = jnp.minimum(jnp.maximum(upslope, jnp.minimum(here, 0.0)), jnp.maximum(here, 0.0))
    return speed * cell + drift * here + limit * limited


def coefficients(row, east, north, kappa, wet, out, first=0):
    here, above = kappa(row), kappa(row + 1)
    wet_here, wet_above = wet(row), wet(row + 1)
    along = face(east(row), here + roll(here, -1), wet_here * roll(wet_here, -1))
    across = face(north(row), here + above, wet_here * wet_above)
    for number, value in enumerate(along + across):
        out[row, number] = value


def advance(source, coef, start, count, store, width=UNROLL):
    def north_flux(row, tracer, cell, diffs):
        return flux(cell, *diffs, tuple(coef[row, 3 + k] for k in range(3)))

    def first_flux(tracer):
        cells = [source(start - 2 + k, tracer) for k in range(4)]
        diffs = [cells[k + 1] - cells[k] for k in range(3)]
        return north_flux(start - 1, tracer, cells[1], diffs)

    def body(number, below):
        base = start + number * width
        below = list(below)
        for tracer in range(2):
            cells = [source(base - 1 + k, tracer) for k in range(width + 3)]
            diffs = [cells[k + 1] - cells[k] for k in range(width + 2)]
            for k in range(width):
                row = base + k
                cell = cells[k + 1]
                here = roll(cell, -1) - cell
                along = flux(
                    cell, roll(here, 1), here, roll(here, -1), tuple(coef[row, i] for i in range(3))
                )
                across = north_flux(row, tracer, cell, diffs[k : k + 3])
                store(row, tracer, cell - (along - roll(along, 1)) - (across - below[tracer]))
                below[tracer] = across
        return tuple(below)

    below = (first_flux(0), first_flux(1))
    if count == width:
        body(0, below)
    else:
        lax.fori_loop(0, count // width, body, below)


def kernel(
    nlon, nlat,
    tracers_hbm, east_hbm, north_hbm, kappa_hbm, levels_hbm, out_ref,
    tracers_in, east_in, north_in, kappa_in, levels,
    cells, wet, to_east, to_west, from_west, from_east, strip,
    main_coef, strip_coef, main_1, main_2, main_3, strip_1, strip_2,
    load_sem, send_sem, recv_sem,
):
    lon, lat = lax.axis_index("lon"), lax.axis_index("lat")
    at_top, at_bottom = lat == nlat - 1, lat == 0
    below_top, above_bottom = jnp.logical_not(at_top), jnp.logical_not(at_bottom)
    east_lon, west_lon = lax.rem(lon + 1, nlon), lax.rem(lon + nlon - 1, nlon)
    fold_lon, fold_east, fold_west = nlon - 1 - lon, nlon - 1 - east_lon, nlon - 1 - west_lon
    east_is_self = jnp.logical_and(at_top, fold_east == lon)
    west_is_self = jnp.logical_and(at_top, fold_west == lon)
    lane = lane_index()

    north_lat = jnp.where(at_top, lat, lat + 1)
    south_lat = jnp.where(at_bottom, lat, lat - 1)
    north = (jnp.where(at_top, fold_lon, lon), north_lat)
    north_east = (jnp.where(at_top, fold_east, east_lon), north_lat)
    north_west = (jnp.where(at_top, fold_west, west_lon), north_lat)
    south, south_east, south_west = (lon, south_lat), (east_lon, south_lat), (west_lon, south_lat)

    partners = (
        ((east_lon, lat), None),
        ((west_lon, lat), None),
        (north, None),
        (north_east, jnp.logical_not(east_is_self)),
        (north_west, jnp.logical_not(west_is_self)),
        (south, above_bottom),
        (south_east, above_bottom),
        (south_west, above_bottom),
    )

    def under(condition, action):
        if condition is None:
            action()
        else:
            pl.when(condition)(action)

    barrier = pltpu.get_barrier_semaphore()
    for device, condition in partners:
        under(
            condition,
            lambda device=device: pl.semaphore_signal(
                barrier, 1, device_id=device, device_id_type=MESH
            ),
        )

    loads = [
        pltpu.make_async_copy(source, target, load_sem.at[number])
        for number, (source, target) in enumerate(
            (
                (levels_hbm, levels.at[pl.ds(PAD, ROWS)]),
                (tracers_hbm, tracers_in),
                (east_hbm, east_in),
                (north_hbm, north_in),
                (kappa_hbm, kappa_in),
            )
        )
    ]
    for copy in loads:
        copy.start()

    @pl.when(at_bottom)
    def _():
        zero = jnp.zeros((LEVELS, COLS), jnp.float32)
        levels[pl.ds(0, PAD)] = jnp.zeros((PAD, COLS), jnp.int32)
        for row in range(PAD - REACH, PAD):
            for number in range(5):
                cells[row, number] = zero
        for number in range(2):
            from_west[number] = zero
            from_east[number] = zero

    for copy in loads:
        copy.wait()

    depth = lax.broadcasted_iota(jnp.int32, (LEVELS, COLS), 0)

    def wet_row(row):
        return (depth < levels[pl.ds(row, 1)]).astype(jnp.float32)

    def gather(number, carry):
        eastern = jnp.zeros((LEVELS, COLS), jnp.float32)
        western = jnp.zeros((LEVELS, COLS), jnp.float32)
        for group in range(4):
            row = number * 4 + group
            values = [
                tracers_in[pl.ds(row, LEVELS, stride=ROWS)],
                tracers_in[pl.ds(row + LEVELS * ROWS, LEVELS, stride=ROWS)],
                east_in[pl.ds(row, LEVELS, stride=ROWS)],
                north_in[pl.ds(row, LEVELS, stride=ROWS)],
                kappa_in[pl.ds(row, LEVELS, stride=ROWS)],
                wet_row(row + PAD),
            ]
            for which in range(5):
                cells[row + PAD, which] = values[which]
            wet[row + PAD] = values[WET]
            for which, (width, end) in enumerate(SLOTS):
                last = 32 * group + end
                inside = jnp.logical_and(lane >= last - width, lane < last)
                eastern = jnp.where(inside, roll(values[which], last), eastern)
                start = 32 * group + 32 - end
                inside = jnp.logical_and(lane >= start, lane < start + width)
                western = jnp.where(inside, roll(values[which], start), western)
        to_east[number] = eastern
        to_west[number] = western
        return carry

    lax.fori_loop(0, ROWS // 4, gather, 0)

    count = 3 + sum(
        condition.astype(jnp.int32) for _, condition in partners if condition is not None
    )
    pl.semaphore_wait(barrier, count)

    own = pl.ds(2, ROWS // 4)
    low, high = pl.ds(0, 2), pl.ds(2 + ROWS // 4, 2)
    top_groups = pl.ds(ROWS // 4 - 2, 2)
    low_rows, high_rows = pl.ds(PAD - REACH, REACH), pl.ds(PAD + ROWS, REACH)
    first_rows, last_rows = pl.ds(PAD, REACH), pl.ds(PAD + ROWS - REACH, REACH)

    def remote(source, target, send, receive, device):
        return pltpu.make_async_remote_copy(
            src_ref=source,
            dst_ref=target,
            send_sem=send_sem.at[send],
            recv_sem=recv_sem.at[receive],
            device_id=device,
            device_id_type=MESH,
        )

    remote(to_east, from_west.at[own], 0, 0, (east_lon, lat)).start()
    remote(to_west, from_east.at[own], 1, 1, (west_lon, lat)).start()

    @pl.when(at_top)
    def _():
        remote(cells.at[last_rows], cells.at[high_rows], 6, 7, north).start()
        remote(levels.at[pl.ds(ROWS, 8)], levels.at[pl.ds(PAD + ROWS, 8)], 8, 9, north).start()

        @pl.when(jnp.logical_not(east_is_self))
        def _():
            remote(to_east.at[top_groups], from_east.at[high], 2, 5, north_east).start()

        @pl.when(jnp.logical_not(west_is_self))
        def _():
            remote(to_west.at[top_groups], from_west.at[high], 3, 4, north_west).start()

        @pl.when(east_is_self)
        def _():
            from_east[high] = to_east[top_groups]

        @pl.when(west_is_self)
        def _():
            from_west[high] = to_west[top_groups]

    @pl.when(below_top)
    def _():
        remote(to_east.at[top_groups], from_west.at[low], 2, 2, north_east).start()
        remote(to_west.at[top_groups], from_east.at[low], 3, 3, north_west).start()

    @pl.when(above_bottom)
    def _():
        remote(to_east.at[low], from_west.at[high], 4, 4, south_east).start()
        remote(to_west.at[low], from_east.at[high], 5, 5, south_west).start()
        remote(levels.at[pl.ds(PAD, 8)], levels.at[pl.ds(PAD + ROWS, 8)], 9, 9, south).start()
        remote(cells.at[first_rows], cells.at[high_rows], 7, 7, south).start()

    @pl.when(below_top)
    def _():
        remote(levels.at[pl.ds(ROWS, 8)], levels.at[pl.ds(0, 8)], 8, 8, north).start()
        remote(cells.at[last_rows], cells.at[low_rows], 6, 6, north).start()


    def folded(value):
        return jnp.where(lane < COLS // 2, roll(value, REACH), roll(value, -REACH))

    def strip_own(number, carry):
        for k in range(2):
            row = PAD + 2 * number + k
            for which in range(5):
                strip[row, which] = folded(cells[row, which])
            strip[row, WET] = folded(wet[row])
        return carry

    lax.fori_loop(0, ROWS // 2, strip_own, 0)

    main_parts = (
        lambda row: cells[row, EAST],
        lambda row: cells[row, NORTH],
        lambda row: cells[row, KAPPA],
        lambda row: wet[row],
    )
    strip_parts = tuple(
        lambda row, which=which: strip[row, which] for which in (EAST, NORTH, KAPPA, WET)
    )

    def main_coefficients(number, carry):
        for k in range(2):
            coefficients(PAD + 2 * number + k, *main_parts, main_coef)
        return carry

    lax.fori_loop(0, ROWS // 2 - 1, main_coefficients, 0)

    def keep(target):
        def store(row, tracer, value):
            target[row, tracer] = value

        return store

    def reading(source):
        return lambda row, tracer: source[row, tracer]

    stages = (reading(cells), reading(main_1), reading(main_2))
    targets = (keep(main_1), keep(main_2), keep(main_3))
    for step in range(3):
        margin = 2 * (step + 1)
        advance(stages[step], main_coef, PAD + margin, ROWS - 2 * margin, targets[step])


    def arrival(slot, target):
        remote(target, target, slot, slot, (lon, lat)).wait_recv()

    def departure(slot, source):
        remote(source, source, slot, slot, (lon, lat)).wait_send()

    arrival(7, cells.at[high_rows])
    arrival(9, levels.at[pl.ds(PAD + ROWS, 8)])
    pl.when(jnp.logical_not(west_is_self))(lambda: arrival(4, from_west.at[high]))
    pl.when(jnp.logical_not(east_is_self))(lambda: arrival(5, from_east.at[high]))

    @pl.when(above_bottom)
    def _():
        arrival(6, cells.at[low_rows])
        arrival(8, levels.at[pl.ds(0, 8)])
        arrival(2, from_west.at[low])
        arrival(3, from_east.at[low])

    arrival(0, from_west.at[own])
    arrival(1, from_east.at[own])

    departure(0, to_east)
    departure(1, to_west)
    pl.when(jnp.logical_not(east_is_self))(lambda: departure(2, to_east.at[top_groups]))
    pl.when(jnp.logical_not(west_is_self))(lambda: departure(3, to_west.at[top_groups]))
    departure(6, cells.at[last_rows])
    departure(8, levels.at[pl.ds(ROWS, 8)])

    @pl.when(above_bottom)
    def _():
        departure(4, to_east.at[low])
        departure(5, to_west.at[low])
        departure(7, cells.at[first_rows])
        departure(9, levels.at[pl.ds(PAD, 8)])

    north_start = PAD + ROWS
    raw_start = jnp.where(at_top, north_start + 2, north_start)
    for k in range(REACH):
        wet[PAD - REACH + k] = wet_row(PAD - REACH + k)
        wet[north_start + k] = wet_row(raw_start + k)

    @pl.when(at_top)
    def _():
        for side in (from_west, from_east):
            lower, upper = side[2 + ROWS // 4], side[3 + ROWS // 4]
            side[2 + ROWS // 4], side[3 + ROWS // 4] = reverse(upper), reverse(lower)

        def swap(k, carry):
            one, other = north_start + k, north_start + REACH - 1 - k
            for which in range(5):
                near, far = cells[one, which], cells[other, which]
                cells[one, which], cells[other, which] = reverse(far), reverse(near)
            near, far = wet[one], wet[other]
            wet[one], wet[other] = reverse(far), reverse(near)
            return carry

        lax.fori_loop(0, REACH // 2, swap, 0)

    def edged(row_group, group, which, value):
        end = SLOTS[which][1]
        left = roll(from_west[row_group], REACH - 32 * group - end)
        right = roll(from_east[row_group], COLS - REACH - 32 - 32 * group + end)
        return jnp.where(lane < REACH, left, jnp.where(lane >= COLS - REACH, right, value))

    def strip_ghost(row_group, groups):
        for group in groups:
            row = 4 * row_group + group
            for which in range(5):
                strip[row, which] = edged(row_group, group, which, folded(cells[row, which]))
            strip[row, WET] = edged(row_group, group, WET, folded(wet[row]))

    strip_ghost(0, (2, 3))
    strip_ghost(1, range(4))
    strip_ghost(2 + ROWS // 4, range(4))
    strip_ghost(3 + ROWS // 4, (0, 1))

    def strip_edges(number, carry):
        row_group = number + 2
        for group in range(4):
            row = 4 * row_group + group
            for which in range(6):
                strip[row, which] = edged(row_group, group, which, strip[row, which])
        return carry

    lax.fori_loop(0, ROWS // 4, strip_edges, 0)

    @pl.when(at_top)
    def _():
        last = north_start - 1
        for part in (cells, strip):
            part[last, NORTH] = 0.5 * (part[last, NORTH] - part[north_start, NORTH])
            for k in range(4):
                row = north_start + k
                part[row, NORTH] = -part[row + 1, NORTH]
                part[row, EAST] = -roll(part[row, EAST], -1)

    for row in (3, 4, 5, 6, 7, 54, 55, 56, 57, 58, 59):
        coefficients(row, *main_parts, main_coef)

    for step in range(3):
        reach = REACH - 2 * (step + 1)
        advance(stages[step], main_coef, PAD - reach, REACH, targets[step], REACH)
        advance(stages[step], main_coef, PAD + ROWS - 2 * (step + 1), REACH, targets[step], REACH)

    def strip_coefficients(number, carry):
        for k in range(3):
            coefficients(3 + 3 * number + k, *strip_parts, strip_coef)
        return carry

    lax.fori_loop(0, 19, strip_coefficients, 0)

    advance(reading(strip), strip_coef, PAD - 4, ROWS + 8, keep(strip_1))
    advance(reading(strip_1), strip_coef, PAD - 2, ROWS + 4, keep(strip_2))

    def finish(row, tracer, value):
        merged = jnp.where(
            lane < REACH,
            roll(value, -REACH),
            jnp.where(lane >= COLS - REACH, roll(value, REACH), main_3[row, tracer]),
        )
        out_ref[pl.ds(tracer * LEVELS * ROWS + row - PAD, LEVELS, stride=ROWS)] = merged

    advance(reading(strip_2), strip_coef, PAD, ROWS, finish)


def per_device(nlon, nlat, tracers, east_courant, north_courant, diffusivity, wet_levels):
    flat = LEVELS * ROWS
    f32 = jnp.float32
    vreg = (LEVELS, COLS)
    result = pl.pallas_call(
        functools.partial(kernel, nlon, nlat),
        out_shape=jax.ShapeDtypeStruct((2 * flat, COLS), f32),
        in_specs=[pl.BlockSpec(memory_space=pltpu.HBM)] * 5,
        out_specs=pl.BlockSpec(memory_space=pltpu.VMEM),
        scratch_shapes=[
            pltpu.VMEM((2 * flat, COLS), f32),
            pltpu.VMEM((flat, COLS), f32),
            pltpu.VMEM((flat, COLS), f32),
            pltpu.VMEM((flat, COLS), f32),
            pltpu.VMEM((SPAN, COLS), jnp.int32),
            pltpu.VMEM((SPAN, 5) + vreg, f32),
            pltpu.VMEM((SPAN,) + vreg, f32),
            pltpu.VMEM((ROWS // 4,) + vreg, f32),
            pltpu.VMEM((ROWS // 4,) + vreg, f32),
            pltpu.VMEM((SPAN // 4,) + vreg, f32),
            pltpu.VMEM((SPAN // 4,) + vreg, f32),
            pltpu.VMEM((SPAN, 6) + vreg, f32),
            pltpu.VMEM((SPAN, 6) + vreg, f32),
            pltpu.VMEM((SPAN, 6) + vreg, f32),
            pltpu.VMEM((SPAN, 2) + vreg, f32),
            pltpu.VMEM((SPAN, 2) + vreg, f32),
            pltpu.VMEM((SPAN, 2) + vreg, f32),
            pltpu.VMEM((SPAN, 2) + vreg, f32),
            pltpu.VMEM((SPAN, 2) + vreg, f32),
            pltpu.SemaphoreType.DMA((5,)),
            pltpu.SemaphoreType.DMA((10,)),
            pltpu.SemaphoreType.DMA((10,)),
        ],
        compiler_params=pltpu.CompilerParams(
            collective_id=0, has_side_effects=True, vmem_limit_bytes=48 << 20
        ),
        name="advect",
    )(
        tracers.reshape(2 * flat, COLS),
        east_courant.reshape(flat, COLS),
        north_courant.reshape(flat, COLS),
        diffusivity.reshape(flat, COLS),
        wet_levels,
    )
    return result.reshape(2, LEVELS, ROWS, COLS)


def solution(mesh):
    placed = (
        P(None, None, "lat", "lon"),
        P(None, "lat", "lon"),
        P(None, "lat", "lon"),
        P(None, "lat", "lon"),
        P("lat", "lon"),
    )
    return jax.shard_map(
        functools.partial(per_device, mesh.shape["lon"], mesh.shape["lat"]),
        mesh=mesh,
        in_specs=placed,
        out_specs=P(None, None, "lat", "lon"),
        check_vma=False,
    )
```

time: 459 us -> 62 us (0.14)
  the two profiles are of different devices: /device:TPU:87 before, /device:TPU:1 now
where the time goes in v1:
time: 62 us; the launch traced here: 61.7 us
  Pallas kernels  56.5 us (91%)
  local copies, waits for them, and re-layouts  5.26 us (8%)
    pallas_call x1, Pallas kernels, per_device(): pl.pallas_call(functools.partial(kernel, nlon, nlat), out_shape=jax.Shape...  56.5 us
    unnamed x11, local copies, waits for them, and re-layouts  5.26 us

profile of v1, /device:TPU:1, one launch (start us, length us, event | category | flops | bytes accessed | tf_op | source)
XLA Modules:
  0.0 61.7 jit_solution(12178695139944076903)
XLA Ops:
  0.0 0.0 copy-start
  0.0 1.0 %copy-done = f32[2,8,48,128]{3,2,1,0:T(8,128)S(1)} copy-done((f32[2,8,48,128]{3,2,1,0:T(8,128)S(1)}, f32[2,8,48,128]{3,2,1,0:T(8,128)}, u32[]{:S(2)}) %copy-start) | copy-done | bytes 393240
  1.0 0.0 copy-start.1
  1.0 0.9 %copy-done.1 = f32[8,48,128]{2,1,0:T(8,128)S(1)} copy-done((f32[8,48,128]{2,1,0:T(8,128)S(1)}, f32[8,48,128]{2,1,0:T(8,128)}, u32[]{:S(2)}) %copy-start.1) | copy-done | bytes 196632
  1.9 0.0 copy-start.2
  1.9 0.9 %copy-done.2 = f32[8,48,128]{2,1,0:T(8,128)S(1)} copy-done((f32[8,48,128]{2,1,0:T(8,128)S(1)}, f32[8,48,128]{2,1,0:T(8,128)}, u32[]{:S(2)}) %copy-start.2) | copy-done | bytes 196632
  2.9 0.0 copy-start.3
  2.9 0.9 %copy-done.3 = f32[8,48,128]{2,1,0:T(8,128)S(1)} copy-done((f32[8,48,128]{2,1,0:T(8,128)S(1)}, f32[8,48,128]{2,1,0:T(8,128)}, u32[]{:S(2)}) %copy-start.3) | copy-done | bytes 196632
  3.8 0.0 copy-start.4
  3.8 0.7 %copy-done.4 = s32[48,128]{1,0:T(8,128)S(1)} copy-done((s32[48,128]{1,0:T(8,128)S(1)}, s32[48,128]{1,0:T(8,128)}, u32[]{:S(2)}) %copy-start.4) | copy-done | bytes 24600
  4.5 56.5 %advect.1 = f32[768,128]{1,0:T(8,128)S(1)} custom-call(f32[768,128]{1,0:T(8,128)S(1)} %bitcast.6, f32[384,128]{1,0:T(8,128)S(1)} %bitcast.7, f32[384,128]{1,0:T(8,128)S(1)} %bitcast.8, f32[384,128]{1,0:T(8,128)S(1)} %bitcast.9, s32[48,128]{1,0:T(8,128)S(1)} %copy-done.4), custom_call_target="tpu_custom_call" | custom-call | tf_op jit(solution)/shard_map/advect/pallas_call | solution.py:443
  61.0 0.7 %copy.7 = f32[2,8,48,128]{3,2,1,0:T(8,128)} copy(f32[2,8,48,128]{3,2,1,0:T(8,128)S(1)} %bitcast.5) | data formatting | bytes 786432
Async XLA Ops:
  0.0 1.0 %copy-start = (f32[2,8,48,128]{3,2,1,0:T(8,128)S(1)}, f32[2,8,48,128]{3,2,1,0:T(8,128)}, u32[]{:S(2)}) copy-start(f32[2,8,48,128]{3,2,1,0:T(8,128)} %param.5) | copy-start | bytes 1179652
  1.0 0.9 %copy-start.1 = (f32[8,48,128]{2,1,0:T(8,128)S(1)}, f32[8,48,128]{2,1,0:T(8,128)}, u32[]{:S(2)}) copy-start(f32[8,48,128]{2,1,0:T(8,128)} %param.6) | copy-start | bytes 589828
  1.9 0.9 %copy-start.2 = (f32[8,48,128]{2,1,0:T(8,128)S(1)}, f32[8,48,128]{2,1,0:T(8,128)}, u32[]{:S(2)}) copy-start(f32[8,48,128]{2,1,0:T(8,128)} %param.7) | copy-start | bytes 589828
  2.9 0.9 %copy-start.3 = (f32[8,48,128]{2,1,0:T(8,128)S(1)}, f32[8,48,128]{2,1,0:T(8,128)}, u32[]{:S(2)}) copy-start(f32[8,48,128]{2,1,0:T(8,128)} %param.8) | copy-start | bytes 589828
  3.8 0.7 %copy-start.4 = (s32[48,128]{1,0:T(8,128)S(1)}, s32[48,128]{1,0:T(8,128)}, u32[]{:S(2)}) copy-start(s32[48,128]{1,0:T(8,128)} %levels_hbm.1) | copy-start | bytes 73732

commit v2 on v1

--- a/solution.py
+++ b/solution.py
@@ -12,7 +12,6 @@
 PAD = 8
 SPAN = ROWS + 2 * PAD
 REACH = 6
-UNROLL = 4
 T0, T1, EAST, NORTH, KAPPA, WET = range(6)
 SLOTS = ((6, 6), (6, 12), (5, 17), (4, 21), (5, 26), (5, 31))
 
@@ -46,7 +45,7 @@
     return speed * cell + drift * here + limit * limited
 
 
-def coefficients(row, east, north, kappa, wet, out, first=0):
+def coefficients(row, east, north, kappa, wet, out):
     here, above = kappa(row), kappa(row + 1)
     wet_here, wet_above = wet(row), wet(row + 1)
     along = face(east(row), here + roll(here, -1), wet_here * roll(wet_here, -1))
@@ -55,7 +54,7 @@
         out[row, number] = value
 
 
-def advance(source, coef, start, count, store, width=UNROLL):
+def advance(source, coef, start, count, store, width):
     def north_flux(row, tracer, cell, diffs):
         return flux(cell, *diffs, tuple(coef[row, 3 + k] for k in range(3)))
 
@@ -173,7 +172,7 @@
     def wet_row(row):
         return (depth < levels[pl.ds(row, 1)]).astype(jnp.float32)
 
-    def gather(number, carry):
+    def gather(number):
         eastern = jnp.zeros((LEVELS, COLS), jnp.float32)
         western = jnp.zeros((LEVELS, COLS), jnp.float32)
         for group in range(4):
@@ -198,9 +197,13 @@
                 western = jnp.where(inside, roll(values[which], start), western)
         to_east[number] = eastern
         to_west[number] = western
+
+    def gather_pair(pair, carry):
+        gather(2 * pair)
+        gather(2 * pair + 1)
         return carry
 
-    lax.fori_loop(0, ROWS // 4, gather, 0)
+    lax.fori_loop(0, ROWS // 8, gather_pair, 0)
 
     count = 3 + sum(
         condition.astype(jnp.int32) for _, condition in partners if condition is not None
@@ -269,14 +272,14 @@
         return jnp.where(lane < COLS // 2, roll(value, REACH), roll(value, -REACH))
 
     def strip_own(number, carry):
-        for k in range(2):
-            row = PAD + 2 * number + k
+        for k in range(8):
+            row = PAD + 8 * number + k
             for which in range(5):
                 strip[row, which] = folded(cells[row, which])
             strip[row, WET] = folded(wet[row])
         return carry
 
-    lax.fori_loop(0, ROWS // 2, strip_own, 0)
+    lax.fori_loop(0, ROWS // 8, strip_own, 0)
 
     main_parts = (
         lambda row: cells[row, EAST],
@@ -289,11 +292,11 @@
     )
 
     def main_coefficients(number, carry):
-        for k in range(2):
-            coefficients(PAD + 2 * number + k, *main_parts, main_coef)
+        for k in range(9):
+            coefficients(PAD + 1 + 9 * number + k, *main_parts, main_coef)
         return carry
 
-    lax.fori_loop(0, ROWS // 2 - 1, main_coefficients, 0)
+    lax.fori_loop(0, 5, main_coefficients, 0)
 
     def keep(target):
         def store(row, tracer, value):
@@ -306,9 +309,9 @@
 
     stages = (reading(cells), reading(main_1), reading(main_2))
     targets = (keep(main_1), keep(main_2), keep(main_3))
-    for step in range(3):
+    for step, width in enumerate((11, 10, 12)):
         margin = 2 * (step + 1)
-        advance(stages[step], main_coef, PAD + margin, ROWS - 2 * margin, targets[step])
+        advance(stages[step], main_coef, PAD + margin, ROWS - 2 * margin, targets[step], width)
 
 
     def arrival(slot, target):
@@ -319,30 +322,13 @@
 
     arrival(7, cells.at[high_rows])
     arrival(9, levels.at[pl.ds(PAD + ROWS, 8)])
-    pl.when(jnp.logical_not(west_is_self))(lambda: arrival(4, from_west.at[high]))
-    pl.when(jnp.logical_not(east_is_self))(lambda: arrival(5, from_east.at[high]))
+    departure(6, cells.at[last_rows])
+    departure(8, levels.at[pl.ds(ROWS, 8)])
 
     @pl.when(above_bottom)
     def _():
         arrival(6, cells.at[low_rows])
         arrival(8, levels.at[pl.ds(0, 8)])
-        arrival(2, from_west.at[low])
-        arrival(3, from_east.at[low])
-
-    arrival(0, from_west.at[own])
-    arrival(1, from_east.at[own])
-
-    departure(0, to_east)
-    departure(1, to_west)
-    pl.when(jnp.logical_not(east_is_self))(lambda: departure(2, to_east.at[top_groups]))
-    pl.when(jnp.logical_not(west_is_self))(lambda: departure(3, to_west.at[top_groups]))
-    departure(6, cells.at[last_rows])
-    departure(8, levels.at[pl.ds(ROWS, 8)])
-
-    @pl.when(above_bottom)
-    def _():
-        departure(4, to_east.at[low])
-        departure(5, to_west.at[low])
         departure(7, cells.at[first_rows])
         departure(9, levels.at[pl.ds(PAD, 8)])
 
@@ -354,10 +340,6 @@
 
     @pl.when(at_top)
     def _():
-        for side in (from_west, from_east):
-            lower, upper = side[2 + ROWS // 4], side[3 + ROWS // 4]
-            side[2 + ROWS // 4], side[3 + ROWS // 4] = reverse(upper), reverse(lower)
-
         def swap(k, carry):
             one, other = north_start + k, north_start + REACH - 1 - k
             for which in range(5):
@@ -369,45 +351,26 @@
 
         lax.fori_loop(0, REACH // 2, swap, 0)
 
-    def edged(row_group, group, which, value):
-        end = SLOTS[which][1]
-        left = roll(from_west[row_group], REACH - 32 * group - end)
-        right = roll(from_east[row_group], COLS - REACH - 32 - 32 * group + end)
-        return jnp.where(lane < REACH, left, jnp.where(lane >= COLS - REACH, right, value))
-
-    def strip_ghost(row_group, groups):
-        for group in groups:
-            row = 4 * row_group + group
+    def strip_ghost(k, carry):
+        for row in (PAD - REACH + k, north_start + k):
             for which in range(5):
-                strip[row, which] = edged(row_group, group, which, folded(cells[row, which]))
-            strip[row, WET] = edged(row_group, group, WET, folded(wet[row]))
-
-    strip_ghost(0, (2, 3))
-    strip_ghost(1, range(4))
-    strip_ghost(2 + ROWS // 4, range(4))
-    strip_ghost(3 + ROWS // 4, (0, 1))
-
-    def strip_edges(number, carry):
-        row_group = number + 2
-        for group in range(4):
-            row = 4 * row_group + group
-            for which in range(6):
-                strip[row, which] = edged(row_group, group, which, strip[row, which])
+                strip[row, which] = folded(cells[row, which])
+            strip[row, WET] = folded(wet[row])
         return carry
 
-    lax.fori_loop(0, ROWS // 4, strip_edges, 0)
-
-    @pl.when(at_top)
-    def _():
+    lax.fori_loop(0, REACH, strip_ghost, 0)
+
+    def fold_speeds(part):
         last = north_start - 1
-        for part in (cells, strip):
-            part[last, NORTH] = 0.5 * (part[last, NORTH] - part[north_start, NORTH])
-            for k in range(4):
-                row = north_start + k
-                part[row, NORTH] = -part[row + 1, NORTH]
-                part[row, EAST] = -roll(part[row, EAST], -1)
-
-    for row in (3, 4, 5, 6, 7, 54, 55, 56, 57, 58, 59):
+        part[last, NORTH] = 0.5 * (part[last, NORTH] - part[north_start, NORTH])
+        for k in range(4):
+            row = north_start + k
+            part[row, NORTH] = -part[row + 1, NORTH]
+            part[row, EAST] = -roll(part[row, EAST], -1)
+
+    pl.when(at_top)(lambda: fold_speeds(cells))
+
+    for row in (3, 4, 5, 6, 7, 8, 54, 55, 56, 57, 58, 59):
         coefficients(row, *main_parts, main_coef)
 
     for step in range(3):
@@ -415,15 +378,64 @@
         advance(stages[step], main_coef, PAD - reach, REACH, targets[step], REACH)
         advance(stages[step], main_coef, PAD + ROWS - 2 * (step + 1), REACH, targets[step], REACH)
 
+    @pl.when(above_bottom)
+    def _():
+        arrival(2, from_west.at[low])
+        arrival(3, from_east.at[low])
+        departure(4, to_east.at[low])
+        departure(5, to_west.at[low])
+
+    @pl.when(jnp.logical_not(west_is_self))
+    def _():
+        arrival(4, from_west.at[high])
+        departure(3, to_west.at[top_groups])
+
+    @pl.when(jnp.logical_not(east_is_self))
+    def _():
+        arrival(5, from_east.at[high])
+        departure(2, to_east.at[top_groups])
+
+    @pl.when(at_top)
+    def _():
+        for side in (from_west, from_east):
+            lower, upper = side[2 + ROWS // 4], side[3 + ROWS // 4]
+            side[2 + ROWS // 4], side[3 + ROWS // 4] = reverse(upper), reverse(lower)
+
+    arrival(0, from_west.at[own])
+    arrival(1, from_east.at[own])
+    departure(0, to_east)
+    departure(1, to_west)
+
+    def edged(row_group, groups):
+        for group in groups:
+            row = 4 * row_group + group
+            for which, (_, end) in enumerate(SLOTS):
+                left = roll(from_west[row_group], REACH - 32 * group - end)
+                right = roll(from_east[row_group], COLS - REACH - 32 - 32 * group + end)
+                strip[row, which] = jnp.where(
+                    lane < REACH, left, jnp.where(lane >= COLS - REACH, right, strip[row, which])
+                )
+
+    def strip_edges(number, carry):
+        edged(1 + 2 * number, range(4))
+        edged(2 + 2 * number, range(4))
+        return carry
+
+    edged(0, (2, 3))
+    lax.fori_loop(0, 7, strip_edges, 0)
+    edged(SPAN // 4 - 1, (0, 1))
+
+    pl.when(at_top)(lambda: fold_speeds(strip))
+
     def strip_coefficients(number, carry):
-        for k in range(3):
-            coefficients(3 + 3 * number + k, *strip_parts, strip_coef)
+        for k in range(19):
+            coefficients(3 + 19 * number + k, *strip_parts, strip_coef)
         return carry
 
-    lax.fori_loop(0, 19, strip_coefficients, 0)
-
-    advance(reading(strip), strip_coef, PAD - 4, ROWS + 8, keep(strip_1))
-    advance(reading(strip_1), strip_coef, PAD - 2, ROWS + 4, keep(strip_2))
+    lax.fori_loop(0, 3, strip_coefficients, 0)
+
+    advance(reading(strip), strip_coef, PAD - 4, ROWS + 8, keep(strip_1), 14)
+    advance(reading(strip_1), strip_coef, PAD - 2, ROWS + 4, keep(strip_2), 13)
 
     def finish(row, tracer, value):
         merged = jnp.where(
@@ -433,7 +445,7 @@
         )
         out_ref[pl.ds(tracer * LEVELS * ROWS + row - PAD, LEVELS, stride=ROWS)] = merged
 
-    advance(reading(strip_2), strip_coef, PAD, ROWS, finish)
+    advance(reading(strip_2), strip_coef, PAD, ROWS, finish, 12)
 
 
 def per_device(nlon, nlat, tracers, east_courant, north_courant, diffusivity, wet_levels):
@@ -442,8 +454,8 @@
     vreg = (LEVELS, COLS)
     result = pl.pallas_call(
         functools.partial(kernel, nlon, nlat),
-        out_shape=jax.ShapeDtypeStruct((2 * flat, COLS), f32),
-        in_specs=[pl.BlockSpec(memory_space=pltpu.HBM)] * 5,
+        out_shape=pltpu.VMEM((2 * flat, COLS), f32),
+        in_specs=[pl.BlockSpec(memory_space=pl.ANY)] * 5,
         out_specs=pl.BlockSpec(memory_space=pltpu.VMEM),
         scratch_shapes=[
             pltpu.VMEM((2 * flat, COLS), f32),
@@ -470,7 +482,7 @@
             pltpu.SemaphoreType.DMA((10,)),
         ],
         compiler_params=pltpu.CompilerParams(
-            collective_id=0, has_side_effects=True, vmem_limit_bytes=48 << 20
+            collective_id=0, has_side_effects=True, vmem_limit_bytes=56 << 20
         ),
         name="advect",
     )(

time: 62 us -> 50.1 us (0.81)
  Pallas kernels: 56.5 us -> 49.2 us
  local copies, waits for them, and re-layouts: 5.26 us -> 0.75 us
    pallas_call x1, Pallas kernels: 56.5 us -> 49.2 us  [per_device(): pl.pallas_call(functools.partial(kernel, nlon, nlat), out_shape=pltpu.VME...]
    unnamed x11 -> x1, local copies, waits for them, and re-layouts: 5.26 us -> 0.75 us
where the time goes in v2:
time: 50.1 us; the launch traced here: 50 us
  Pallas kernels  49.2 us (98%)
  local copies, waits for them, and re-layouts  0.75 us (1%)
    pallas_call x1, Pallas kernels, per_device(): pl.pallas_call(functools.partial(kernel, nlon, nlat), out_shape=pltpu.VME...  49.2 us

profile of v2, /device:TPU:1, one launch (start us, length us, event | category | flops | bytes accessed | tf_op | source)
XLA Modules:
  0.0 50.0 jit_solution(5896938249692169143)
XLA Ops:
  0.0 49.2 %advect.1 = f32[768,128]{1,0:T(8,128)S(1)} custom-call(f32[768,128]{1,0:T(8,128)} %bitcast.6, f32[384,128]{1,0:T(8,128)} %bitcast.7, f32[384,128]{1,0:T(8,128)} %bitcast.8, f32[384,128]{1,0:T(8,128)} %bitcast.9, s32[48,128]{1,0:T(8,128)} %levels_hbm.1), custom_call_target="tpu_custom_call" | custom-call | tf_op jit(solution)/shard_map/advect/pallas_call | solution.py:455
  49.2 0.7 %copy.7 = f32[2,8,48,128]{3,2,1,0:T(8,128)} copy(f32[2,8,48,128]{3,2,1,0:T(8,128)S(1)} %bitcast.5) | data formatting | bytes 786432

commit v3 on v2

--- a/solution.py
+++ b/solution.py
@@ -12,6 +12,9 @@
 PAD = 8
 SPAN = ROWS + 2 * PAD
 REACH = 6
+GROUPS, LANES = 4, 32
+STRIDE = ROWS // GROUPS
+STRIPS = STRIDE + 2 * REACH
 T0, T1, EAST, NORTH, KAPPA, WET = range(6)
 SLOTS = ((6, 6), (6, 12), (5, 17), (4, 21), (5, 26), (5, 31))
 
@@ -92,8 +95,8 @@
     nlon, nlat,
     tracers_hbm, east_hbm, north_hbm, kappa_hbm, levels_hbm, out_ref,
     tracers_in, east_in, north_in, kappa_in, levels,
-    cells, wet, to_east, to_west, from_west, from_east, strip,
-    main_coef, strip_coef, main_1, main_2, main_3, strip_1, strip_2,
+    cells, wet, to_east, to_west, corner_east, corner_west, from_west, from_east, strip,
+    main_coef, strip_coef, main_1, main_2, main_3, strip_in, strip_1, strip_2,
     load_sem, send_sem, recv_sem,
 ):
     lon, lat = lax.axis_index("lon"), lax.axis_index("lat")
@@ -175,8 +178,8 @@
     def gather(number):
         eastern = jnp.zeros((LEVELS, COLS), jnp.float32)
         western = jnp.zeros((LEVELS, COLS), jnp.float32)
-        for group in range(4):
-            row = number * 4 + group
+        for group in range(GROUPS):
+            row = number + STRIDE * group
             values = [
                 tracers_in[pl.ds(row, LEVELS, stride=ROWS)],
                 tracers_in[pl.ds(row + LEVELS * ROWS, LEVELS, stride=ROWS)],
@@ -189,10 +192,10 @@
                 cells[row + PAD, which] = values[which]
             wet[row + PAD] = values[WET]
             for which, (width, end) in enumerate(SLOTS):
-                last = 32 * group + end
+                last = LANES * group + end
                 inside = jnp.logical_and(lane >= last - width, lane < last)
                 eastern = jnp.where(inside, roll(values[which], last), eastern)
-                start = 32 * group + 32 - end
+                start = LANES * (group + 1) - end
                 inside = jnp.logical_and(lane >= start, lane < start + width)
                 western = jnp.where(inside, roll(values[which], start), western)
         to_east[number] = eastern
@@ -203,16 +206,24 @@
         gather(2 * pair + 1)
         return carry
 
-    lax.fori_loop(0, ROWS // 8, gather_pair, 0)
+    lax.fori_loop(0, STRIDE // 2, gather_pair, 0)
+
+    for side, corner in ((to_east, corner_east), (to_west, corner_west)):
+        for number, rows in enumerate((range(0, 4), range(4, 6), range(ROWS - 6, ROWS - 4), range(ROWS - 4, ROWS))):
+            packed = side[rows[0] % STRIDE]
+            for row in rows:
+                moved = roll(side[row % STRIDE], LANES * (row % GROUPS - row // STRIDE))
+                packed = jnp.where(lane // LANES == row % GROUPS, moved, packed)
+            corner[number] = packed
 
     count = 3 + sum(
         condition.astype(jnp.int32) for _, condition in partners if condition is not None
     )
     pl.semaphore_wait(barrier, count)
 
-    own = pl.ds(2, ROWS // 4)
-    low, high = pl.ds(0, 2), pl.ds(2 + ROWS // 4, 2)
-    top_groups = pl.ds(ROWS // 4 - 2, 2)
+    own = pl.ds(2, STRIDE)
+    low, high = pl.ds(0, 2), pl.ds(2 + STRIDE, 2)
+    high_corner = pl.ds(2, 2)
     low_rows, high_rows = pl.ds(PAD - REACH, REACH), pl.ds(PAD + ROWS, REACH)
     first_rows, last_rows = pl.ds(PAD, REACH), pl.ds(PAD + ROWS - REACH, REACH)
 
@@ -236,29 +247,29 @@
 
         @pl.when(jnp.logical_not(east_is_self))
         def _():
-            remote(to_east.at[top_groups], from_east.at[high], 2, 5, north_east).start()
+            remote(corner_east.at[high_corner], from_east.at[high], 2, 5, north_east).start()
 
         @pl.when(jnp.logical_not(west_is_self))
         def _():
-            remote(to_west.at[top_groups], from_west.at[high], 3, 4, north_west).start()
+            remote(corner_west.at[high_corner], from_west.at[high], 3, 4, north_west).start()
 
         @pl.when(east_is_self)
         def _():
-            from_east[high] = to_east[top_groups]
+            from_east[high] = corner_east[high_corner]
 
         @pl.when(west_is_self)
         def _():
-            from_west[high] = to_west[top_groups]
+            from_west[high] = corner_west[high_corner]
 
     @pl.when(below_top)
     def _():
-        remote(to_east.at[top_groups], from_west.at[low], 2, 2, north_east).start()
-        remote(to_west.at[top_groups], from_east.at[low], 3, 3, north_west).start()
+        remote(corner_east.at[high_corner], from_west.at[low], 2, 2, north_east).start()
+        remote(corner_west.at[high_corner], from_east.at[low], 3, 3, north_west).start()
 
     @pl.when(above_bottom)
     def _():
-        remote(to_east.at[low], from_west.at[high], 4, 4, south_east).start()
-        remote(to_west.at[low], from_east.at[high], 5, 5, south_west).start()
+        remote(corner_east.at[low], from_west.at[high], 4, 4, south_east).start()
+        remote(corner_west.at[low], from_east.at[high], 5, 5, south_west).start()
         remote(levels.at[pl.ds(PAD, 8)], levels.at[pl.ds(PAD + ROWS, 8)], 9, 9, south).start()
         remote(cells.at[first_rows], cells.at[high_rows], 7, 7, south).start()
 
@@ -268,18 +279,35 @@
         remote(cells.at[last_rows], cells.at[low_rows], 6, 6, north).start()
 
 
-    def folded(value):
-        return jnp.where(lane < COLS // 2, roll(value, REACH), roll(value, -REACH))
+    group_lane = lane % LANES
+    left_halo, right_halo = group_lane < REACH, group_lane >= LANES - REACH
+    to_left, to_right = REACH, LANES - REACH
+
+    def edges(value, group):
+        return jnp.where(
+            lane < LANES * group + LANES // 2,
+            roll(value, LANES * group + to_left),
+            roll(value, LANES * group + to_right),
+        )
+
+    def packed_rows(read):
+        total = edges(read(0), 0)
+        for group in range(1, GROUPS):
+            total = jnp.where(lane // LANES == group, edges(read(group), group), total)
+        return total
 
     def strip_own(number, carry):
-        for k in range(8):
-            row = PAD + 8 * number + k
+        for k in range(2):
+            first = PAD + 2 * number + k
+            target = REACH + 2 * number + k
             for which in range(5):
-                strip[row, which] = folded(cells[row, which])
-            strip[row, WET] = folded(wet[row])
+                strip[target, which] = packed_rows(
+                    lambda group, which=which: cells[first + STRIDE * group, which]
+                )
+            strip[target, WET] = packed_rows(lambda group: wet[first + STRIDE * group])
         return carry
 
-    lax.fori_loop(0, ROWS // 8, strip_own, 0)
+    lax.fori_loop(0, STRIDE // 2, strip_own, 0)
 
     main_parts = (
         lambda row: cells[row, EAST],
@@ -352,23 +380,28 @@
         lax.fori_loop(0, REACH // 2, swap, 0)
 
     def strip_ghost(k, carry):
-        for row in (PAD - REACH + k, north_start + k):
-            for which in range(5):
-                strip[row, which] = folded(cells[row, which])
-            strip[row, WET] = folded(wet[row])
+        for which in range(6):
+            def read(row, which=which):
+                return wet[row] if which == WET else cells[row, which]
+
+            below = roll(strip[STRIDE + k, which], LANES)
+            strip[k, which] = jnp.where(lane < LANES, edges(read(PAD - REACH + k), 0), below)
+            above = roll(strip[REACH + k, which], -LANES)
+            strip[REACH + STRIDE + k, which] = jnp.where(
+                lane >= COLS - LANES, edges(read(north_start + k), GROUPS - 1), above
+            )
         return carry
 
     lax.fori_loop(0, REACH, strip_ghost, 0)
 
-    def fold_speeds(part):
-        last = north_start - 1
-        part[last, NORTH] = 0.5 * (part[last, NORTH] - part[north_start, NORTH])
-        for k in range(4):
-            row = north_start + k
-            part[row, NORTH] = -part[row + 1, NORTH]
-            part[row, EAST] = -roll(part[row, EAST], -1)
-
-    pl.when(at_top)(lambda: fold_speeds(cells))
+    def fold_speeds(part, last, where):
+        part[last, NORTH] = where(0.5 * (part[last, NORTH] - part[last + 1, NORTH]), part[last, NORTH])
+        for k in range(1, 5):
+            row = last + k
+            part[row, NORTH] = where(-part[row + 1, NORTH], part[row, NORTH])
+            part[row, EAST] = where(-roll(part[row, EAST], -1), part[row, EAST])
+
+    pl.when(at_top)(lambda: fold_speeds(cells, north_start - 1, lambda new, old: new))
 
     for row in (3, 4, 5, 6, 7, 8, 54, 55, 56, 57, 58, 59):
         coefficients(row, *main_parts, main_coef)
@@ -378,74 +411,120 @@
         advance(stages[step], main_coef, PAD - reach, REACH, targets[step], REACH)
         advance(stages[step], main_coef, PAD + ROWS - 2 * (step + 1), REACH, targets[step], REACH)
 
+    def inner(k, carry):
+        for tracer in range(2):
+            near = packed_rows(lambda group: main_1[PAD + k + STRIDE * group, tracer])
+            strip_in[REACH + k, tracer] = near
+        return carry
+
+    lax.fori_loop(0, STRIDE, inner, 0)
+    for k in range(4):
+        for tracer in range(2):
+            strip_in[2 + k, tracer] = jnp.where(
+                lane < LANES,
+                edges(main_1[PAD - 4 + k, tracer], 0),
+                roll(strip_in[STRIDE + 2 + k, tracer], LANES),
+            )
+            strip_in[REACH + STRIDE + k, tracer] = jnp.where(
+                lane >= COLS - LANES,
+                edges(main_1[north_start + k, tracer], GROUPS - 1),
+                roll(strip_in[REACH + k, tracer], -LANES),
+            )
+
     @pl.when(above_bottom)
     def _():
         arrival(2, from_west.at[low])
         arrival(3, from_east.at[low])
-        departure(4, to_east.at[low])
-        departure(5, to_west.at[low])
+        departure(4, corner_east.at[low])
+        departure(5, corner_west.at[low])
 
     @pl.when(jnp.logical_not(west_is_self))
     def _():
         arrival(4, from_west.at[high])
-        departure(3, to_west.at[top_groups])
+        departure(3, corner_west.at[high_corner])
 
     @pl.when(jnp.logical_not(east_is_self))
     def _():
         arrival(5, from_east.at[high])
-        departure(2, to_east.at[top_groups])
+        departure(2, corner_east.at[high_corner])
 
     @pl.when(at_top)
     def _():
         for side in (from_west, from_east):
-            lower, upper = side[2 + ROWS // 4], side[3 + ROWS // 4]
-            side[2 + ROWS // 4], side[3 + ROWS // 4] = reverse(upper), reverse(lower)
+            lower, upper = side[2 + STRIDE], side[3 + STRIDE]
+            side[2 + STRIDE], side[3 + STRIDE] = reverse(upper), reverse(lower)
 
     arrival(0, from_west.at[own])
     arrival(1, from_east.at[own])
     departure(0, to_east)
     departure(1, to_west)
 
-    def edged(row_group, groups):
-        for group in groups:
-            row = 4 * row_group + group
-            for which, (_, end) in enumerate(SLOTS):
-                left = roll(from_west[row_group], REACH - 32 * group - end)
-                right = roll(from_east[row_group], COLS - REACH - 32 - 32 * group + end)
-                strip[row, which] = jnp.where(
-                    lane < REACH, left, jnp.where(lane >= COLS - REACH, right, strip[row, which])
+    def halo(number, shift, which):
+        end = SLOTS[which][1]
+        return jnp.where(
+            left_halo,
+            roll(from_west[number], shift + REACH - end),
+            roll(from_east[number], shift + end - REACH),
+        )
+
+    outside = jnp.logical_or(left_halo, right_halo)
+
+    def strip_edges(number, carry):
+        for k in range(6):
+            place = 6 * number + k
+            for which in range(6):
+                strip[REACH + place, which] = jnp.where(
+                    outside, halo(2 + place, 0, which), strip[REACH + place, which]
                 )
-
-    def strip_edges(number, carry):
-        edged(1 + 2 * number, range(4))
-        edged(2 + 2 * number, range(4))
         return carry
 
-    edged(0, (2, 3))
-    lax.fori_loop(0, 7, strip_edges, 0)
-    edged(SPAN // 4 - 1, (0, 1))
-
-    pl.when(at_top)(lambda: fold_speeds(strip))
-
-    def strip_coefficients(number, carry):
-        for k in range(19):
-            coefficients(3 + 19 * number + k, *strip_parts, strip_coef)
-        return carry
-
-    lax.fori_loop(0, 3, strip_coefficients, 0)
-
-    advance(reading(strip), strip_coef, PAD - 4, ROWS + 8, keep(strip_1), 14)
-    advance(reading(strip_1), strip_coef, PAD - 2, ROWS + 4, keep(strip_2), 13)
-
-    def finish(row, tracer, value):
-        merged = jnp.where(
-            lane < REACH,
-            roll(value, -REACH),
-            jnp.where(lane >= COLS - REACH, roll(value, REACH), main_3[row, tracer]),
+    lax.fori_loop(0, STRIDE // 6, strip_edges, 0)
+
+    for k in range(REACH):
+        for which in range(6):
+            corner = halo((2 + k) // 4, -LANES * ((2 + k) % 4), which)
+            below = halo(2 + STRIDE - REACH + k, LANES, which)
+            strip[k, which] = jnp.where(
+                outside, jnp.where(lane < LANES, corner, below), strip[k, which]
+            )
+            corner = halo(2 + STRIDE + k // 4, LANES * (GROUPS - 1 - k % 4), which)
+            above = halo(2 + k, -LANES, which)
+            place = REACH + STRIDE + k
+            strip[place, which] = jnp.where(
+                outside, jnp.where(lane >= COLS - LANES, corner, above), strip[place, which]
+            )
+
+    @pl.when(at_top)
+    def _():
+        fold_speeds(
+            strip, REACH + STRIDE - 1, lambda new, old: jnp.where(lane >= COLS - LANES, new, old)
         )
-        out_ref[pl.ds(tracer * LEVELS * ROWS + row - PAD, LEVELS, stride=ROWS)] = merged
-
-    advance(reading(strip_2), strip_coef, PAD, ROWS, finish, 12)
+
+    for place in range(1, STRIPS - 2):
+        coefficients(place, *strip_parts, strip_coef)
+
+    lost = jnp.logical_and(group_lane >= LANES // 2 - 2, group_lane < LANES // 2 + 2)
+
+    def first_store(place, tracer, value):
+        strip_1[place, tracer] = jnp.where(lost, strip_in[place, tracer], value)
+
+    def finish(place, tracer, value):
+        for group in range(GROUPS):
+            row = place - REACH + STRIDE * group
+            merged = jnp.where(
+                lane < REACH,
+                roll(value, -LANES * group - to_left),
+                jnp.where(
+                    lane >= COLS - REACH,
+                    roll(value, -LANES * group - to_right),
+                    main_3[row + PAD, tracer],
+                ),
+            )
+            out_ref[pl.ds(tracer * LEVELS * ROWS + row, LEVELS, stride=ROWS)] = merged
+
+    advance(reading(strip), strip_coef, 2, STRIPS - 4, first_store, 10)
+    advance(reading(strip_1), strip_coef, 4, STRIPS - 8, keep(strip_2), 8)
+    advance(reading(strip_2), strip_coef, REACH, STRIDE, finish, 6)
 
 
 def per_device(nlon, nlat, tracers, east_courant, north_courant, diffusivity, wet_levels):
@@ -465,18 +544,21 @@
             pltpu.VMEM((SPAN, COLS), jnp.int32),
             pltpu.VMEM((SPAN, 5) + vreg, f32),
             pltpu.VMEM((SPAN,) + vreg, f32),
-            pltpu.VMEM((ROWS // 4,) + vreg, f32),
-            pltpu.VMEM((ROWS // 4,) + vreg, f32),
-            pltpu.VMEM((SPAN // 4,) + vreg, f32),
-            pltpu.VMEM((SPAN // 4,) + vreg, f32),
+            pltpu.VMEM((STRIDE,) + vreg, f32),
+            pltpu.VMEM((STRIDE,) + vreg, f32),
+            pltpu.VMEM((4,) + vreg, f32),
+            pltpu.VMEM((4,) + vreg, f32),
+            pltpu.VMEM((STRIDE + 4,) + vreg, f32),
+            pltpu.VMEM((STRIDE + 4,) + vreg, f32),
+            pltpu.VMEM((STRIPS, 6) + vreg, f32),
             pltpu.VMEM((SPAN, 6) + vreg, f32),
-            pltpu.VMEM((SPAN, 6) + vreg, f32),
-            pltpu.VMEM((SPAN, 6) + vreg, f32),
+            pltpu.VMEM((STRIPS, 6) + vreg, f32),
             pltpu.VMEM((SPAN, 2) + vreg, f32),
             pltpu.VMEM((SPAN, 2) + vreg, f32),
             pltpu.VMEM((SPAN, 2) + vreg, f32),
-            pltpu.VMEM((SPAN, 2) + vreg, f32),
-            pltpu.VMEM((SPAN, 2) + vreg, f32),
+            pltpu.VMEM((STRIPS, 2) + vreg, f32),
+            pltpu.VMEM((STRIPS, 2) + vreg, f32),
+            pltpu.VMEM((STRIPS, 2) + vreg, f32),
             pltpu.SemaphoreType.DMA((5,)),
             pltpu.SemaphoreType.DMA((10,)),
             pltpu.SemaphoreType.DMA((10,)),

time: 50.1 us -> 48.7 us (0.972)
  Pallas kernels: 49.2 us -> 47.8 us
    pallas_call x1, Pallas kernels: 49.2 us -> 47.8 us  [per_device(): pl.pallas_call(functools.partial(kernel, nlon, nlat), out_shape=pltpu.VME...]
where the time goes in v3:
time: 48.7 us; the launch traced here: 48.5 us
  Pallas kernels  47.8 us (98%)
  local copies, waits for them, and re-layouts  0.75 us (2%)
    pallas_call x1, Pallas kernels, per_device(): pl.pallas_call(functools.partial(kernel, nlon, nlat), out_shape=pltpu.VME...  47.8 us

profile of v3, /device:TPU:1, one launch (start us, length us, event | category | flops | bytes accessed | tf_op | source)
XLA Modules:
  0.0 48.5 jit_solution(16581743417130028434)
XLA Ops:
  0.0 47.8 %advect.1 = f32[768,128]{1,0:T(8,128)S(1)} custom-call(f32[768,128]{1,0:T(8,128)} %bitcast.6, f32[384,128]{1,0:T(8,128)} %bitcast.7, f32[384,128]{1,0:T(8,128)} %bitcast.8, f32[384,128]{1,0:T(8,128)} %bitcast.9, s32[48,128]{1,0:T(8,128)} %levels_hbm.1), custom_call_target="tpu_custom_call" | custom-call | tf_op jit(solution)/shard_map/advect/pallas_call | solution.py:534
  47.8 0.7 %copy.7 = f32[2,8,48,128]{3,2,1,0:T(8,128)} copy(f32[2,8,48,128]{3,2,1,0:T(8,128)S(1)} %bitcast.5) | data formatting | bytes 786432

commit v4 on v3

--- a/solution.py
+++ b/solution.py
@@ -96,7 +96,7 @@
     tracers_hbm, east_hbm, north_hbm, kappa_hbm, levels_hbm, out_ref,
     tracers_in, east_in, north_in, kappa_in, levels,
     cells, wet, to_east, to_west, corner_east, corner_west, from_west, from_east, strip,
-    main_coef, strip_coef, main_1, main_2, main_3, strip_in, strip_1, strip_2,
+    main_coef, strip_coef, main_1, main_2, main_3, strip_in, strip_1, strip_2, top_speed,
     load_sem, send_sem, recv_sem,
 ):
     lon, lat = lax.axis_index("lon"), lax.axis_index("lat")
@@ -163,9 +163,8 @@
         for row in range(PAD - REACH, PAD):
             for number in range(5):
                 cells[row, number] = zero
-        for number in range(2):
-            from_west[number] = zero
-            from_east[number] = zero
+        from_west[0] = zero
+        from_east[0] = zero
 
     for copy in loads:
         copy.wait()
@@ -209,7 +208,7 @@
     lax.fori_loop(0, STRIDE // 2, gather_pair, 0)
 
     for side, corner in ((to_east, corner_east), (to_west, corner_west)):
-        for number, rows in enumerate((range(0, 4), range(4, 6), range(ROWS - 6, ROWS - 4), range(ROWS - 4, ROWS))):
+        for number, rows in enumerate((range(GROUPS), range(ROWS - GROUPS, ROWS))):
             packed = side[rows[0] % STRIDE]
             for row in rows:
                 moved = roll(side[row % STRIDE], LANES * (row % GROUPS - row // STRIDE))
@@ -221,9 +220,9 @@
     )
     pl.semaphore_wait(barrier, count)
 
-    own = pl.ds(2, STRIDE)
-    low, high = pl.ds(0, 2), pl.ds(2 + STRIDE, 2)
-    high_corner = pl.ds(2, 2)
+    own = pl.ds(1, STRIDE)
+    low, high = pl.ds(0, 1), pl.ds(1 + STRIDE, 1)
+    high_corner = pl.ds(1, 1)
     low_rows, high_rows = pl.ds(PAD - REACH, REACH), pl.ds(PAD + ROWS, REACH)
     first_rows, last_rows = pl.ds(PAD, REACH), pl.ds(PAD + ROWS - REACH, REACH)
 
@@ -270,13 +269,19 @@
     def _():
         remote(corner_east.at[low], from_west.at[high], 4, 4, south_east).start()
         remote(corner_west.at[low], from_east.at[high], 5, 5, south_west).start()
-        remote(levels.at[pl.ds(PAD, 8)], levels.at[pl.ds(PAD + ROWS, 8)], 9, 9, south).start()
-        remote(cells.at[first_rows], cells.at[high_rows], 7, 7, south).start()
-
-    @pl.when(below_top)
-    def _():
-        remote(levels.at[pl.ds(ROWS, 8)], levels.at[pl.ds(0, 8)], 8, 8, north).start()
-        remote(cells.at[last_rows], cells.at[low_rows], 6, 6, north).start()
+
+    def send_rows():
+        @pl.when(above_bottom)
+        def _():
+            remote(levels.at[pl.ds(PAD, 8)], levels.at[pl.ds(PAD + ROWS, 8)], 9, 9, south).start()
+            remote(cells.at[first_rows], cells.at[high_rows], 7, 7, south).start()
+
+        @pl.when(below_top)
+        def _():
+            remote(levels.at[pl.ds(ROWS, 8)], levels.at[pl.ds(0, 8)], 8, 8, north).start()
+            remote(cells.at[last_rows], cells.at[low_rows], 6, 6, north).start()
+
+    send_rows()
 
 
     group_lane = lane % LANES
@@ -350,15 +355,11 @@
 
     arrival(7, cells.at[high_rows])
     arrival(9, levels.at[pl.ds(PAD + ROWS, 8)])
-    departure(6, cells.at[last_rows])
-    departure(8, levels.at[pl.ds(ROWS, 8)])
 
     @pl.when(above_bottom)
     def _():
         arrival(6, cells.at[low_rows])
         arrival(8, levels.at[pl.ds(0, 8)])
-        departure(7, cells.at[first_rows])
-        departure(9, levels.at[pl.ds(PAD, 8)])
 
     north_start = PAD + ROWS
     raw_start = jnp.where(at_top, north_start + 2, north_start)
@@ -384,27 +385,27 @@
             def read(row, which=which):
                 return wet[row] if which == WET else cells[row, which]
 
-            below = roll(strip[STRIDE + k, which], LANES)
-            strip[k, which] = jnp.where(lane < LANES, edges(read(PAD - REACH + k), 0), below)
-            above = roll(strip[REACH + k, which], -LANES)
-            strip[REACH + STRIDE + k, which] = jnp.where(
-                lane >= COLS - LANES, edges(read(north_start + k), GROUPS - 1), above
-            )
+            strip[k, which] = edges(read(PAD - REACH + k), 0)
+            strip[REACH + STRIDE + k, which] = edges(read(north_start + k), GROUPS - 1)
         return carry
 
     lax.fori_loop(0, REACH, strip_ghost, 0)
 
-    def fold_speeds(part, last, where):
-        part[last, NORTH] = where(0.5 * (part[last, NORTH] - part[last + 1, NORTH]), part[last, NORTH])
-        for k in range(1, 5):
-            row = last + k
-            part[row, NORTH] = where(-part[row + 1, NORTH], part[row, NORTH])
-            part[row, EAST] = where(-roll(part[row, EAST], -1), part[row, EAST])
-
-    pl.when(at_top)(lambda: fold_speeds(cells, north_start - 1, lambda new, old: new))
-
-    for row in (3, 4, 5, 6, 7, 8, 54, 55, 56, 57, 58, 59):
+    top_speed[...] = cells[north_start - 1, NORTH]
+
+    @pl.when(at_top)
+    def _():
+        top_speed[...] = 0.5 * (top_speed[...] - cells[north_start, NORTH])
+        for k in range(4):
+            row = north_start + k
+            cells[row, NORTH] = -cells[row + 1, NORTH]
+            cells[row, EAST] = -roll(cells[row, EAST], -1)
+
+    for row in (3, 4, 5, 6, 7, 8, 54, 56, 57, 58, 59):
         coefficients(row, *main_parts, main_coef)
+    coefficients(
+        north_start - 1, main_parts[0], lambda row: top_speed[...], *main_parts[2:], main_coef
+    )
 
     for step in range(3):
         reach = REACH - 2 * (step + 1)
@@ -435,29 +436,17 @@
     def _():
         arrival(2, from_west.at[low])
         arrival(3, from_east.at[low])
-        departure(4, corner_east.at[low])
-        departure(5, corner_west.at[low])
-
-    @pl.when(jnp.logical_not(west_is_self))
-    def _():
-        arrival(4, from_west.at[high])
-        departure(3, corner_west.at[high_corner])
-
-    @pl.when(jnp.logical_not(east_is_self))
-    def _():
-        arrival(5, from_east.at[high])
-        departure(2, corner_east.at[high_corner])
+
+    pl.when(jnp.logical_not(west_is_self))(lambda: arrival(4, from_west.at[high]))
+    pl.when(jnp.logical_not(east_is_self))(lambda: arrival(5, from_east.at[high]))
 
     @pl.when(at_top)
     def _():
         for side in (from_west, from_east):
-            lower, upper = side[2 + STRIDE], side[3 + STRIDE]
-            side[2 + STRIDE], side[3 + STRIDE] = reverse(upper), reverse(lower)
+            side[1 + STRIDE] = reverse(side[1 + STRIDE])
 
     arrival(0, from_west.at[own])
     arrival(1, from_east.at[own])
-    departure(0, to_east)
-    departure(1, to_west)
 
     def halo(number, shift, which):
         end = SLOTS[which][1]
@@ -474,31 +463,37 @@
             place = 6 * number + k
             for which in range(6):
                 strip[REACH + place, which] = jnp.where(
-                    outside, halo(2 + place, 0, which), strip[REACH + place, which]
+                    outside, halo(1 + place, 0, which), strip[REACH + place, which]
                 )
         return carry
 
     lax.fori_loop(0, STRIDE // 6, strip_edges, 0)
 
     for k in range(REACH):
+        place = REACH + STRIDE + k
         for which in range(6):
-            corner = halo((2 + k) // 4, -LANES * ((2 + k) % 4), which)
-            below = halo(2 + STRIDE - REACH + k, LANES, which)
-            strip[k, which] = jnp.where(
-                outside, jnp.where(lane < LANES, corner, below), strip[k, which]
+            lowest, highest = strip[k, which], strip[place, which]
+            if k >= REACH - GROUPS:
+                corner = halo(0, -LANES * (k - REACH + GROUPS), which)
+                lowest = jnp.where(outside, corner, lowest)
+            if k < GROUPS:
+                corner = halo(1 + STRIDE, LANES * (GROUPS - 1 - k), which)
+                highest = jnp.where(outside, corner, highest)
+            strip[k, which] = jnp.where(lane < LANES, lowest, roll(strip[STRIDE + k, which], LANES))
+            strip[place, which] = jnp.where(
+                lane >= COLS - LANES, highest, roll(strip[REACH + k, which], -LANES)
             )
-            corner = halo(2 + STRIDE + k // 4, LANES * (GROUPS - 1 - k % 4), which)
-            above = halo(2 + k, -LANES, which)
-            place = REACH + STRIDE + k
-            strip[place, which] = jnp.where(
-                outside, jnp.where(lane >= COLS - LANES, corner, above), strip[place, which]
-            )
 
     @pl.when(at_top)
     def _():
-        fold_speeds(
-            strip, REACH + STRIDE - 1, lambda new, old: jnp.where(lane >= COLS - LANES, new, old)
-        )
+        top_group = lane >= COLS - LANES
+        last = REACH + STRIDE - 1
+        north = strip[last, NORTH]
+        strip[last, NORTH] = jnp.where(top_group, 0.5 * (north - strip[last + 1, NORTH]), north)
+        for place in range(last + 1, last + 5):
+            north, east = strip[place, NORTH], strip[place, EAST]
+            strip[place, NORTH] = jnp.where(top_group, -strip[place + 1, NORTH], north)
+            strip[place, EAST] = jnp.where(top_group, -roll(east, -1), east)
 
     for place in range(1, STRIPS - 2):
         coefficients(place, *strip_parts, strip_coef)
@@ -525,6 +520,20 @@
     advance(reading(strip), strip_coef, 2, STRIPS - 4, first_store, 10)
     advance(reading(strip_1), strip_coef, 4, STRIPS - 8, keep(strip_2), 8)
     advance(reading(strip_2), strip_coef, REACH, STRIDE, finish, 6)
+
+    departure(0, to_east)
+    departure(1, to_west)
+    pl.when(jnp.logical_not(east_is_self))(lambda: departure(2, corner_east.at[high_corner]))
+    pl.when(jnp.logical_not(west_is_self))(lambda: departure(3, corner_west.at[high_corner]))
+    departure(6, cells.at[last_rows])
+    departure(8, levels.at[pl.ds(ROWS, 8)])
+
+    @pl.when(above_bottom)
+    def _():
+        departure(4, corner_east.at[low])
+        departure(5, corner_west.at[low])
+        departure(7, cells.at[first_rows])
+        departure(9, levels.at[pl.ds(PAD, 8)])
 
 
 def per_device(nlon, nlat, tracers, east_courant, north_courant, diffusivity, wet_levels):
@@ -546,10 +555,10 @@
             pltpu.VMEM((SPAN,) + vreg, f32),
             pltpu.VMEM((STRIDE,) + vreg, f32),
             pltpu.VMEM((STRIDE,) + vreg, f32),
-            pltpu.VMEM((4,) + vreg, f32),
-            pltpu.VMEM((4,) + vreg, f32),
-            pltpu.VMEM((STRIDE + 4,) + vreg, f32),
-            pltpu.VMEM((STRIDE + 4,) + vreg, f32),
+            pltpu.VMEM((2,) + vreg, f32),
+            pltpu.VMEM((2,) + vreg, f32),
+            pltpu.VMEM((STRIDE + 2,) + vreg, f32),
+            pltpu.VMEM((STRIDE + 2,) + vreg, f32),
             pltpu.VMEM((STRIPS, 6) + vreg, f32),
             pltpu.VMEM((SPAN, 6) + vreg, f32),
             pltpu.VMEM((STRIPS, 6) + vreg, f32),
@@ -559,6 +568,7 @@
             pltpu.VMEM((STRIPS, 2) + vreg, f32),
             pltpu.VMEM((STRIPS, 2) + vreg, f32),
             pltpu.VMEM((STRIPS, 2) + vreg, f32),
+            pltpu.VMEM(vreg, f32),
             pltpu.SemaphoreType.DMA((5,)),
             pltpu.SemaphoreType.DMA((10,)),
             pltpu.SemaphoreType.DMA((10,)),

time: 48.7 us -> 47.2 us (0.969)
  Pallas kernels: 47.8 us -> 46.2 us
    pallas_call x1, Pallas kernels: 47.8 us -> 46.2 us  [per_device(): pl.pallas_call(functools.partial(kernel, nlon, nlat), out_shape=pltpu.VME...]
where the time goes in v4:
time: 47.2 us; the launch traced here: 47 us
  Pallas kernels  46.2 us (98%)
  local copies, waits for them, and re-layouts  0.75 us (2%)
    pallas_call x1, Pallas kernels, per_device(): pl.pallas_call(functools.partial(kernel, nlon, nlat), out_shape=pltpu.VME...  46.2 us

profile of v4, /device:TPU:1, one launch (start us, length us, event | category | flops | bytes accessed | tf_op | source)
XLA Modules:
  0.0 47.0 jit_solution(12267554613561383971)
XLA Ops:
  0.0 46.2 %advect.1 = f32[768,128]{1,0:T(8,128)S(1)} custom-call(f32[768,128]{1,0:T(8,128)} %bitcast.6, f32[384,128]{1,0:T(8,128)} %bitcast.7, f32[384,128]{1,0:T(8,128)} %bitcast.8, f32[384,128]{1,0:T(8,128)} %bitcast.9, s32[48,128]{1,0:T(8,128)} %levels_hbm.1), custom_call_target="tpu_custom_call" | custom-call | tf_op jit(solution)/shard_map/advect/pallas_call | solution.py:543
  46.2 0.7 %copy.7 = f32[2,8,48,128]{3,2,1,0:T(8,128)} copy(f32[2,8,48,128]{3,2,1,0:T(8,128)S(1)} %bitcast.5) | data formatting | bytes 786432

commit v5 on v4

--- a/solution.py
+++ b/solution.py
@@ -223,8 +223,16 @@
     own = pl.ds(1, STRIDE)
     low, high = pl.ds(0, 1), pl.ds(1 + STRIDE, 1)
     high_corner = pl.ds(1, 1)
-    low_rows, high_rows = pl.ds(PAD - REACH, REACH), pl.ds(PAD + ROWS, REACH)
-    first_rows, last_rows = pl.ds(PAD, REACH), pl.ds(PAD + ROWS - REACH, REACH)
+    inner_count, both = REACH - 1, pl.ds(0, 2)
+
+    def part(inner, outer):
+        return cells.at[pl.ds(inner, inner_count)], cells.at[pl.ds(outer, 1), both]
+
+    first_rows = part(PAD, PAD + inner_count)
+    last_rows = part(PAD + ROWS - inner_count, PAD + ROWS - REACH)
+    low_rows = part(PAD - inner_count, PAD - REACH)
+    high_rows = part(PAD + ROWS, PAD + ROWS + inner_count)
+    fold_rows = part(PAD + ROWS + 1, PAD + ROWS)
 
     def remote(source, target, send, receive, device):
         return pltpu.make_async_remote_copy(
@@ -241,7 +249,8 @@
 
     @pl.when(at_top)
     def _():
-        remote(cells.at[last_rows], cells.at[high_rows], 6, 7, north).start()
+        for k in range(2):
+            remote(last_rows[k], fold_rows[k], 6 + 4 * k, 7 + 4 * k, north).start()
         remote(levels.at[pl.ds(ROWS, 8)], levels.at[pl.ds(PAD + ROWS, 8)], 8, 9, north).start()
 
         @pl.when(jnp.logical_not(east_is_self))
@@ -274,12 +283,14 @@
         @pl.when(above_bottom)
         def _():
             remote(levels.at[pl.ds(PAD, 8)], levels.at[pl.ds(PAD + ROWS, 8)], 9, 9, south).start()
-            remote(cells.at[first_rows], cells.at[high_rows], 7, 7, south).start()
+            for k in range(2):
+                remote(first_rows[k], high_rows[k], 7 + 4 * k, 7 + 4 * k, south).start()
 
         @pl.when(below_top)
         def _():
             remote(levels.at[pl.ds(ROWS, 8)], levels.at[pl.ds(0, 8)], 8, 8, north).start()
-            remote(cells.at[last_rows], cells.at[low_rows], 6, 6, north).start()
+            for k in range(2):
+                remote(last_rows[k], low_rows[k], 6 + 4 * k, 6 + 4 * k, north).start()
 
     send_rows()
 
@@ -353,12 +364,22 @@
     def departure(slot, source):
         remote(source, source, slot, slot, (lon, lat)).wait_send()
 
-    arrival(7, cells.at[high_rows])
+    @pl.when(at_top)
+    def _():
+        for k in range(2):
+            arrival(7 + 4 * k, fold_rows[k])
+
+    @pl.when(below_top)
+    def _():
+        for k in range(2):
+            arrival(7 + 4 * k, high_rows[k])
+
     arrival(9, levels.at[pl.ds(PAD + ROWS, 8)])
 
     @pl.when(above_bottom)
     def _():
-        arrival(6, cells.at[low_rows])
+        for k in range(2):
+            arrival(6 + 4 * k, low_rows[k])
         arrival(8, levels.at[pl.ds(0, 8)])
 
     north_start = PAD + ROWS
@@ -525,14 +546,16 @@
     departure(1, to_west)
     pl.when(jnp.logical_not(east_is_self))(lambda: departure(2, corner_east.at[high_corner]))
     pl.when(jnp.logical_not(west_is_self))(lambda: departure(3, corner_west.at[high_corner]))
-    departure(6, cells.at[last_rows])
+    for k in range(2):
+        departure(6 + 4 * k, last_rows[k])
     departure(8, levels.at[pl.ds(ROWS, 8)])
 
     @pl.when(above_bottom)
     def _():
         departure(4, corner_east.at[low])
         departure(5, corner_west.at[low])
-        departure(7, cells.at[first_rows])
+        for k in range(2):
+            departure(7 + 4 * k, first_rows[k])
         departure(9, levels.at[pl.ds(PAD, 8)])
 
 
@@ -570,8 +593,8 @@
             pltpu.VMEM((STRIPS, 2) + vreg, f32),
             pltpu.VMEM(vreg, f32),
             pltpu.SemaphoreType.DMA((5,)),
-            pltpu.SemaphoreType.DMA((10,)),
-            pltpu.SemaphoreType.DMA((10,)),
+            pltpu.SemaphoreType.DMA((12,)),
+            pltpu.SemaphoreType.DMA((12,)),
         ],
         compiler_params=pltpu.CompilerParams(
             collective_id=0, has_side_effects=True, vmem_limit_bytes=56 << 20

time: 47.2 us -> 46.9 us (level)
  no operation moved by 1% of the time
where the time goes in v5:
time: 46.9 us; the launch traced here: 46.8 us
  Pallas kernels  46 us (98%)
  local copies, waits for them, and re-layouts  0.75 us (2%)
    pallas_call x1, Pallas kernels, per_device(): pl.pallas_call(functools.partial(kernel, nlon, nlat), out_shape=pltpu.VME...  46 us

profile of v5, /device:TPU:1, one launch (start us, length us, event | category | flops | bytes accessed | tf_op | source)
XLA Modules:
  0.0 46.8 jit_solution(5543500127605724569)
XLA Ops:
  0.0 46.0 %advect.1 = f32[768,128]{1,0:T(8,128)S(1)} custom-call(f32[768,128]{1,0:T(8,128)} %bitcast.6, f32[384,128]{1,0:T(8,128)} %bitcast.7, f32[384,128]{1,0:T(8,128)} %bitcast.8, f32[384,128]{1,0:T(8,128)} %bitcast.9, s32[48,128]{1,0:T(8,128)} %levels_hbm.1), custom_call_target="tpu_custom_call" | custom-call | tf_op jit(solution)/shard_map/advect/pallas_call | solution.py:566
  46.0 0.7 %copy.7 = f32[2,8,48,128]{3,2,1,0:T(8,128)} copy(f32[2,8,48,128]{3,2,1,0:T(8,128)S(1)} %bitcast.5) | data formatting | bytes 786432
